TPU v7x, 32 devices: a whole 2x2x4 slice. The times are simulated.
32 devices in a mesh: mix: 4 (over z), fsdp: 4 (over y, x), tile: 2 (over core).
Axes of the slice: x: 2, y: 2, z: 4, core: 2. Of those that a mesh axis runs over, the one named last changes fastest.
Arguments:
- video: bfloat16 [16, 8, 8, 8, 256], P(('mix', 'fsdp'), 'tile'), parts along dimension 0
- conv_weight: bfloat16 [1024, 6912], P(('mix', 'fsdp')), parts along dimension 0, may hold values from -0.078125 to 0.078125
- down_weight: bfloat16 [1024, 2304], P(('mix', 'fsdp')), parts along dimension 0, may hold values from -0.125 to 0.125
- out_grad: bfloat16 [16, 8, 4, 4, 256], P(('mix', 'fsdp'), 'tile'), parts along dimension 0, may hold values from -6 to 6
- clip_bucket: int32 [16], P(('mix', 'fsdp')), parts along dimension 0, may hold values from 0 to 3
- start_frame: int32 [16], P(('mix', 'fsdp')), parts along dimension 0, may hold values from 0 to 4
- bucket_res: int32 [4, 2], replicated, may hold values from 4 to 8, as said below
Outputs:
- down: bfloat16 [16, 8, 4, 4, 256], P(('mix', 'fsdp'), 'tile'), parts along dimension 0
- video_grad: bfloat16 [16, 8, 8, 8, 256], P(('mix', 'fsdp'), 'tile'), parts along dimension 0
- conv_weight_grad: float32 [1024, 6912], P(('mix', 'fsdp')), parts along dimension 0
- down_weight_grad: float32 [1024, 2304], P(('mix', 'fsdp')), parts along dimension 0
There are 4 independent parts, one for each index of `mix`. A program takes and returns all parts, laid end to end along the dimension named above; an argument that names none is the same for every part. Nothing has to cross between parts.
Inputs may be any that keep to these rules, and one draw needn't show every extreme that they name: `start_frame`: frames before it are padding. `bucket_res`: valid rows (column 0) and columns (column 1) per bucket; no two buckets have the same pair.
All inputs are finite; a program needn't handle non-finite values.
Results may differ from a plain program's by a relative error of at most 0.0051.
Values may be sent and summed in bfloat16 or wider, within the bound.
A program may use at most 128 MiB of HBM per device.

v0:
```python
import jax
import jax.numpy as jnp
from jax import lax
from jax.sharding import PartitionSpec as P

GROUPS = 32


EPSILON = 1e-06


def shifted(block, axis, distance):
    devices = range(lax.axis_size(axis))
    route = [(i - distance, i) for i in devices if i - distance in devices]
    return lax.ppermute(block, axis, route)


def valid_mask(clip_bucket, start_frame, bucket_res, first_frame, frame_count, side_cells):
    bucket_ids = jnp.arange(bucket_res.shape[0], dtype=jnp.int32)
    picked = (clip_bucket[:, None] == bucket_ids[None, :]).astype(jnp.int32)
    limits = jnp.sum(picked[:, :, None] * bucket_res[None, :, :], axis=1)
    frame_ids = first_frame + jnp.arange(frame_count, dtype=jnp.int32)
    positions = jnp.arange(side_cells, dtype=jnp.int32)
    in_time = frame_ids[None, :] >= start_frame[:, None]
    in_rows = positions[None, :] < limits[:, 0:1]
    in_cols = positions[None, :] < limits[:, 1:2]
    inside = in_time[:, :, None, None] & in_rows[:, None, :, None] & in_cols[:, None, None, :]
    return (inside.astype(jnp.float32)[..., None], limits)


def time_group(padded, tap_time, out_frames, side_cells, flipped):
    channel_count = padded.shape[-1]
    time_start = 2 - tap_time if flipped else tap_time
    layers = []
    for tap_row in range(3):
        for tap_col in range(3):
            row_start = 2 - tap_row if flipped else tap_row
            col_start = 2 - tap_col if flipped else tap_col
            window = padded[
                :,
                time_start : time_start + out_frames,
                row_start : row_start + side_cells,
                col_start : col_start + side_cells,
                :,
            ]
            layers.append(window.reshape(-1, channel_count))
    return jnp.stack(layers)


def stride_taps(padded, side_cells):
    channel_count = padded.shape[-1]
    layers = []
    for tap_row in range(3):
        for tap_col in range(3):
            window = padded[
                :, :, tap_row : tap_row + side_cells : 2, tap_col : tap_col + side_cells : 2, :
            ]
            layers.append(window.reshape(-1, channel_count))
    return jnp.stack(layers)


def weight_terms(grad_rows, slabs, cot_rows, hidden_padded, frame_count, side_cells):
    out_rows = grad_rows.shape[1]
    down_term = lax.dot_general(
        grad_rows, slabs, (((0,), (1,)), ((), ())), preferred_element_type=jnp.float32
    ).reshape(out_rows, -1)
    conv_parts = []
    for tap_time in range(3):
        group = time_group(hidden_padded, tap_time, frame_count, side_cells, False)
        conv_parts.append(
            lax.dot_general(
                cot_rows, group, (((0,), (1,)), ((), ())), preferred_element_type=jnp.float32
            )
        )
    conv_term = jnp.concatenate(conv_parts, axis=1).reshape(out_rows, -1)
    return (conv_term, down_term)


def transpose_conv(grad_padded, conv_weight, out_frames, side_cells):
    channel_count = grad_padded.shape[-1]
    row_total = grad_padded.shape[0] * out_frames * side_cells * side_cells
    initial = jnp.zeros((row_total, channel_count), jnp.float32)
    running = initial
    weight_panel = lax.all_gather(conv_weight, "fsdp", axis=0, tiled=True)
    panel_rows = weight_panel.shape[0]
    panel = weight_panel.reshape(panel_rows, 27, channel_count)
    for tap_time in range(3):
        group = time_group(grad_padded, tap_time, out_frames, side_cells, True)
        running = running + lax.dot_general(
            group,
            panel[:, 9 * tap_time : 9 * tap_time + 9, :],
            (((0, 2), (1, 0)), ((), ())),
            preferred_element_type=jnp.float32,
        )
    return running


def shards(video, conv_weight, down_weight, out_grad, clip_bucket, start_frame, bucket_res):
    clip_count, frame_count, side_cells, side_again, channel_count = video.shape
    half_side = side_cells // 2
    group_width = channel_count // GROUPS
    tiles = lax.axis_size("tile")
    mask, limits = valid_mask(
        clip_bucket,
        start_frame,
        bucket_res,
        lax.axis_index("tile") * frame_count,
        frame_count,
        side_cells,
    )
    valid_count = (
        (frame_count * tiles - start_frame) * limits[:, 0] * limits[:, 1] * group_width
    ).astype(jnp.float32)
    grouped_shape = (clip_count, frame_count, side_cells, side_cells, GROUPS, group_width)
    summed_axes = (1, 2, 3, 5)
    cell_weight = mask[..., None]
    grouped = video.astype(jnp.float32).reshape(grouped_shape)
    first_sum = lax.psum(jnp.sum(grouped * cell_weight, axis=summed_axes), "tile")
    centre = first_sum / valid_count[:, None]
    offset = grouped - centre[:, None, None, None, :, None]
    second_sum = lax.psum(jnp.sum(cell_weight * offset * offset, axis=summed_axes), "tile")
    spread = second_sum / valid_count[:, None]
    inverse = lax.rsqrt(spread + EPSILON)
    normed_grouped = offset * inverse[:, None, None, None, :, None]
    normed = normed_grouped.reshape(video.shape)
    hidden = (mask * jax.nn.silu(normed)).astype(jnp.bfloat16)
    past = shifted(hidden[:, frame_count - 2 :], "tile", 1)
    hidden_padded = jnp.pad(
        jnp.concatenate([past, hidden], axis=1), ((0, 0), (0, 0), (1, 1), (1, 1), (0, 0))
    )

    def conv_columns(weight_panel):
        panel = weight_panel.reshape(weight_panel.shape[0], 27, channel_count)
        summed = None
        for tap_time in range(3):
            group = time_group(hidden_padded, tap_time, frame_count, side_cells, False)
            term = lax.dot_general(
                group,
                panel[:, 9 * tap_time : 9 * tap_time + 9, :],
                (((0, 2), (1, 2)), ((), ())),
                preferred_element_type=jnp.float32,
            )
            summed = term if summed is None else summed + term
        return summed

    conv_out = conv_columns(lax.all_gather(conv_weight, "fsdp", axis=0, tiled=True))
    residual = (mask * (video.astype(jnp.float32) + conv_out.reshape(video.shape))).astype(
        jnp.bfloat16
    )
    down_slabs = stride_taps(
        jnp.pad(residual, ((0, 0), (0, 0), (0, 1), (0, 1), (0, 0))), side_cells
    )
    weight_panel = lax.all_gather(down_weight, "fsdp", axis=0, tiled=True)
    panel = weight_panel.reshape(weight_panel.shape[0], 9, channel_count)
    down_out = lax.dot_general(
        down_slabs, panel, (((0, 2), (1, 2)), ((), ())), preferred_element_type=jnp.float32
    )
    down = down_out.astype(jnp.bfloat16).reshape(
        clip_count, frame_count, half_side, half_side, channel_count
    )
    grad_flat = out_grad.reshape(-1, channel_count)
    weight_panel = lax.all_gather(down_weight, "fsdp", axis=0, tiled=True)
    panel_rows = weight_panel.shape[0]
    panel = weight_panel.reshape(panel_rows, 9, channel_count)
    tap_grads = lax.dot_general(
        grad_flat, panel, (((1,), (0,)), ((), ())), preferred_element_type=jnp.float32
    )
    spread_back = jnp.zeros(
        (clip_count, frame_count, side_cells + 1, side_cells + 1, channel_count), jnp.float32
    )
    for tap_row in range(3):
        for tap_col in range(3):
            term = tap_grads[:, tap_row * 3 + tap_col, :].reshape(
                clip_count, frame_count, half_side, half_side, channel_count
            )
            spread_back = spread_back.at[
                :, :, tap_row : tap_row + side_cells : 2, tap_col : tap_col + side_cells : 2, :
            ].add(term)
    res_grad = (mask * spread_back[:, :, :side_cells, :side_cells, :]).astype(jnp.bfloat16)
    res_flat = res_grad.reshape(-1, channel_count)
    later = shifted(res_grad[:, :2], "tile", -1)
    grad_padded = jnp.pad(
        jnp.concatenate([res_grad, later], axis=1), ((0, 0), (0, 0), (1, 1), (1, 1), (0, 0))
    )
    back_hidden = transpose_conv(grad_padded, conv_weight, frame_count, side_cells).reshape(
        video.shape
    )
    gate_value = jax.nn.sigmoid(normed)
    pushed = mask * back_hidden * gate_value * (1.0 + normed * (1.0 - gate_value))
    pushed_grouped = pushed.reshape(grouped_shape)
    push_sum, pair_sum = lax.psum(
        (
            jnp.sum(pushed_grouped, axis=summed_axes),
            jnp.sum(pushed_grouped * normed_grouped, axis=summed_axes),
        ),
        "tile",
    )
    mean_push = push_sum / valid_count[:, None]
    mean_pair = pair_sum / valid_count[:, None]
    through_norm = inverse[:, None, None, None, :, None] * (
        pushed_grouped
        - mean_push[:, None, None, None, :, None]
        - normed_grouped * mean_pair[:, None, None, None, :, None]
    )
    video_grad = (mask * through_norm.reshape(video.shape) + res_grad.astype(jnp.float32)).astype(
        jnp.bfloat16
    )
    conv_term, down_term = weight_terms(
        grad_flat, down_slabs, res_flat, hidden_padded, frame_count, side_cells
    )
    conv_share, down_share = (
        lax.psum_scatter(conv_term, ("fsdp", "tile"), scatter_dimension=0, tiled=True),
        lax.psum_scatter(down_term, ("fsdp", "tile"), scatter_dimension=0, tiled=True),
    )
    conv_weight_grad, down_weight_grad = (
        lax.all_gather(conv_share, "tile", axis=0, tiled=True),
        lax.all_gather(down_share, "tile", axis=0, tiled=True),
    )
    return (down, video_grad, conv_weight_grad, down_weight_grad)


def solution(mesh):
    placed = (
        P(("mix", "fsdp"), "tile", None, None, None),
        P(("mix", "fsdp"), None),
        P(("mix", "fsdp"), None),
        P(("mix", "fsdp"), "tile", None, None, None),
        P(("mix", "fsdp")),
        P(("mix", "fsdp")),
        P(),
    )
    return jax.shard_map(
        shards,
        mesh=mesh,
        in_specs=placed,
        out_specs=(
            P(("mix", "fsdp"), "tile", None, None, None),
            P(("mix", "fsdp"), "tile", None, None, None),
            P(("mix", "fsdp"), None),
            P(("mix", "fsdp"), None),
        ),
        check_vma=False,
    )
```

profile of v0, /device:TPU:0, one launch (start us, length us, event | category | flops | bytes accessed | tf_op | source)
XLA Modules:
  0.0 257.3 jit_solution(14554759923453696010)
XLA Ops:
  14.8 2.6 %psum.28 = f32[1,32]{1,0:T(1,128)S(1)} all-reduce(f32[1,32]{1,0:T(1,128)S(1)} %bitcast.278), channel_id=1, replica_groups=mesh['mix'=4,'fsdp'=4,'tile'=2] {'tile'}, use_global_device_ids=true, to_apply=%region_3.0 | all-reduce | flops 32 | bytes 256 | tf_op jit(solution)/shard_map/psum | solution.py:118
  17.6 22.8 %all-gather.6.cloned.1.call-done = bf16[256,2304]{1,0:T(8,128)(2,1)} async-done(((bf16[64,2304]{1,0:T(8,128)(2,1)}), bf16[256,2304]{1,0:T(8,128)(2,1)}) %all-gather.6.cloned.1.call-update) | async-done | bytes 1179664 | tf_op jit(solution)/shard_map/all_gather | solution.py:153
  40.3 1.6 copy.274
  47.3 1.3 scatter_fusion.3
  48.6 1.3 scatter_fusion.4
  57.0 3.4 %psum.29 = f32[1,32]{1,0:T(1,128)S(1)} all-reduce(f32[1,32]{1,0:T(1,128)S(1)} %bitcast.276), channel_id=1, replica_groups=mesh['mix'=4,'fsdp'=4,'tile'=2] {'tile'}, use_global_device_ids=true, to_apply=%region_6.7 | all-reduce | flops 32 | bytes 256 | tf_op jit(solution)/shard_map/psum | solution.py:121
  67.6 21.9 %all-gather.4.cloned.1.call-done = bf16[256,6912]{1,0:T(8,128)(2,1)} async-done(((bf16[64,6912]{1,0:T(8,128)(2,1)}), bf16[256,6912]{1,0:T(8,128)(2,1)}) %all-gather.4.cloned.1.call-update) | async-done | bytes 3538960 | tf_op jit(solution)/shard_map/all_gather | solution.py:146
  89.5 6.0 %copy.270 = bf16[256,6912]{0,1:T(8,128)(2,1)} copy(bf16[256,6912]{1,0:T(8,128)(2,1)} %all-gather.4.cloned.1.call-done) | data formatting | bytes 7077888 | tf_op jit(solution)/shard_map/all_gather | solution.py:146
  95.4 1.8 convolution_bitcast_fusion.1
  97.2 2.2 convolution_bitcast_fusion
  99.5 1.8 fusion.3
  101.9 2.5 all-reduce.3
  105.5 2.1 collective-permute-start
  112.2 3.2 %pad_maximum_fusion = f32[256,27,256]{0,2,1:T(8,128)} fusion(f32[256,9,256]{0,2,1:T(8,128)S(1)} %fusion.54, f32[256,9,256]{0,2,1:T(8,128)S(1)} %fusion.53, f32[256,9,256]{0,2,1:T(8,128)S(1)} %fusion.52), kind=kLoop, calls=%fused_computation.9 | loop fusion | flops 3538944 | bytes 14155776 | tf_op jit(solution)/shard_map/concatenate | solution.py:75
  115.4 8.5 %copy.290 = f32[256,6912]{1,0:T(8,128)} copy(f32[256,6912]{0,1:T(8,128)} %bitcast.187) | data formatting | bytes 14155776 | tf_op jit(solution)/shard_map/reshape | solution.py:75
  124.0 2.2 convolution_bitcast_fusion.4
  126.2 1.7 convolution_bitcast_fusion.3
  127.9 1.7 fusion.1
  135.9 2.0 copy.291
  138.0 51.5 %reduce-scatter.3.cloned.1.call-done = f32[32,6912]{1,0:T(8,128)} async-done(((f32[256,6912]{1,0:T(8,128)}), f32[32,6912]{1,0:T(8,128)}) %reduce-scatter.3.cloned.1.call-update) | async-done | bytes 884752 | tf_op jit(solution)/shard_map/reduce_scatter | solution.py:212
  190.6 45.1 %reduce-scatter.5.cloned.1.call-done = f32[32,2304]{1,0:T(8,128)} async-done(((f32[256,2304]{1,0:T(8,128)}), f32[32,2304]{1,0:T(8,128)}) %reduce-scatter.5.cloned.1.call-update) | async-done | bytes 294928 | tf_op jit(solution)/shard_map/reduce_scatter | solution.py:213
  235.7 2.4 all_gather.17
  238.1 9.1 %all-gather.8.cloned.1.call-done = f32[64,6912]{1,0:T(8,128)} async-done(((f32[32,6912]{1,0:T(8,128)}), f32[64,6912]{1,0:T(8,128)}) %all-gather.8.cloned.1.call-update) | async-done | bytes 1769488 | tf_op jit(solution)/shard_map/all_gather | solution.py:216
  247.2 2.8 %copy.371 = f32[64,6912]{1,0:T(8,128)} copy(f32[64,6912]{1,0:T(8,128)} %all-gather.8.cloned.1.call-done) | data formatting | bytes 3538944
  (216 shorter events, 38.3 us)
Async XLA Ops:
  7.2 2.9 %copy-start.12 = (s32[4,2]{0,1:T(2,128)S(1)}, s32[4,2]{0,1:T(2,128)}, u32[]{:S(2)}) copy-start(s32[4,2]{0,1:T(2,128)} %param.13) | copy-start | bytes 100
  7.2 7.3 %copy-start = (bf16[1,4,8,8,256]{4,3,2,1,0:T(8,128)(2,1)S(1)}, bf16[1,4,8,8,256]{4,3,2,1,0:T(8,128)(2,1)}, u32[]{:S(2)}) copy-start(bf16[1,4,8,8,256]{4,3,2,1,0:T(8,128)(2,1)} %param.7) | copy-start | bytes 393220
  7.2 10.3 %copy-start.9 = (bf16[1,4,4,4,256]{4,3,2,1,0:T(4,128)(2,1)S(1)}, bf16[1,4,4,4,256]{4,3,2,1,0:T(4,128)(2,1)}, u32[]{:S(2)}) copy-start(bf16[1,4,4,4,256]{4,3,2,1,0:T(4,128)(2,1)} %param.10) | copy-start | bytes 98308
  7.2 33.1 %all-gather.6.cloned.1.call-start = ((), (), s32[]{:S(2)}) async-start(), calls=%async_computation.3 | async-start | bytes 1474560 | tf_op jit(solution)/shard_map/all_gather | solution.py:153
  7.9 81.5 %all-gather.4.cloned.1.call-start = ((), (), s32[]{:S(2)}) async-start(), calls=%async_computation.2 | async-start | bytes 4423680 | tf_op jit(solution)/shard_map/all_gather | solution.py:146
  8.7 180.9 %reduce-scatter.3.cloned.1.call-start = ((), (), s32[]{:S(2)}) async-start(), calls=%async_computation.4 | async-start | bytes 7962624 | tf_op jit(solution)/shard_map/reduce_scatter | solution.py:212
  17.6 24.3 %copy-start.8 = (bf16[64,256,1]{1,0,2:T(8,128)(2,1)}, bf16[64,256,1]{1,0,2:T(8,128)(2,1)S(1)}, u32[]{:S(2)}) copy-start(bf16[64,256,1]{1,0,2:T(8,128)(2,1)S(1)} %reshape.350) | copy-start | bytes 98308
  55.7 4.9 %collective-permute-start.1 = (bf16[1,2,8,8,256]{4,3,2,1,0:T(8,128)(2,1)S(1)}, bf16[1,2,8,8,256]{4,3,2,1,0:T(8,128)(2,1)S(1)}, u32[]{:S(2)}, u32[]{:S(2)}) collective-permute-start(bf16[1,2,8,8,256]{4,3,2,1,0:T(8,128)(2,1)S(1)} %slice.406), channel_id=1, source_target_pairs={{1,0},{3,2},{5,4},{7,6},{9,8},{11,10},{13,12},{15,14},{17,16},{19,... | collective-permute-start | bytes 196616 | tf_op jit(solution)/shard_map/ppermute | solution.py:15
  61.9 1.0 copy-start.4
  62.1 4.9 %copy-start.10 = (bf16[9,256,256]{2,1,0:T(8,128)(2,1)}, bf16[9,256,256]{2,1,0:T(8,128)(2,1)S(1)}, u32[]{:S(2)}) copy-start(bf16[9,256,256]{2,1,0:T(8,128)(2,1)S(1)} %constant_dynamic-update-slice_fusion.45) | copy-start | bytes 3538948
  67.6 27.8 %copy-start.11 = (bf16[9,256,256]{2,1,0:T(8,128)(2,1)S(1)}, bf16[9,256,256]{2,1,0:T(8,128)(2,1)}, u32[]{:S(2)}) copy-start(bf16[9,256,256]{2,1,0:T(8,128)(2,1)} %copy-done.10) | copy-start | bytes 3538948
  97.2 2.2 copy-start.5
  105.5 3.0 %collective-permute-start = (bf16[1,2,8,8,256]{4,3,2,1,0:T(8,128)(2,1)S(1)}, bf16[1,2,8,8,256]{4,3,2,1,0:T(8,128)(2,1)S(1)}, u32[]{:S(2)}, u32[]{:S(2)}) collective-permute-start(bf16[1,2,8,8,256]{4,3,2,1,0:T(8,128)(2,1)S(1)} %slice.388), channel_id=1, source_target_pairs={{0,1},{2,3},{4,5},{6,7},{8,9},{10,11},{12,13},{14,15},{16,17},{18,... | collective-permute-start | bytes 196616 | tf_op jit(solution)/shard_map/ppermute | solution.py:15
  109.3 1.2 copy-start.3
  110.6 1.0 copy-start.1
  123.9 111.8 %reduce-scatter.5.cloned.1.call-start = ((), (), s32[]{:S(2)}) async-start(), calls=%async_computation.6 | async-start | bytes 2654208 | tf_op jit(solution)/shard_map/reduce_scatter | solution.py:213
  123.9 2.2 copy-start.2
  134.6 1.3 copy-start.6
  138.0 51.7 %copy-start.7 = (bf16[9,64,256]{2,1,0:T(8,128)(2,1)S(1)}, bf16[9,64,256]{2,1,0:T(8,128)(2,1)}, u32[]{:S(2)}) copy-start(bf16[9,64,256]{2,1,0:T(8,128)(2,1)} %copy-done.6) | copy-start | bytes 884740
  138.0 109.2 %all-gather.8.cloned.1.call-start = ((), (), s32[]{:S(2)}) async-start(), calls=%async_computation.5 | async-start | bytes 2654208 | tf_op jit(solution)/shard_map/all_gather | solution.py:216
Sparse Core Ops, SparseCore 0:
  9.9 30.4 all-gather.5
  42.2 47.2 all-gather.3
  124.0 65.5 reduce-scatter.2
  193.2 42.4 reduce-scatter.4
  237.1 10.0 all-gather.7
where the time goes:
time: 258 us; the launch traced here: 257 us
  waiting for transfers between devices  153 us (59%)
  local copies, waits for them, and re-layouts  38.5 us (15%)
  other arithmetic  18.7 us (7%)
  between operations  17.6 us (7%)
  matrix products  15.4 us (6%)
  blocking collectives  10.9 us (4%)
  starting transfers between devices  3.55 us (1%)
    reduce_scatter x1, waiting for transfers between devices, shards(): lax.psum_scatter(conv_term, ('fsdp', 'tile'), scatter_dimension=0, tiled=...  51.5 us
    reduce_scatter x1, waiting for transfers between devices, shards(): lax.psum_scatter(down_term, ('fsdp', 'tile'), scatter_dimension=0, tiled=...  45.1 us
    all_gather x1, waiting for transfers between devices, shards(): weight_panel = lax.all_gather(down_weight, 'fsdp', axis=0, tiled=True)  22.8 us
    all_gather x1, waiting for transfers between devices, shards(): lax.all_gather(conv_weight, 'fsdp', axis=0, tiled=True)  21.9 us
    scatter-add x9, other arithmetic, shards(): spread_back = spread_back.at[:, :, tap_row:tap_row + side_cells:2, tap_co...  11.9 us
    unnamed x84, local copies, waits for them, and re-layouts  10.7 us
    all_gather x1, waiting for transfers between devices, shards(): lax.all_gather(conv_share, 'tile', axis=0, tiled=True)  9.09 us
    reshape x1, local copies, waits for them, and re-layouts, weight_terms(): conv_term = jnp.concatenate(conv_parts, axis=1).reshape(out_rows, -1)  8.47 us
  transfers between devices with their start and end apart: 7, of which 6 were waited for; matrix products, arithmetic and copies ran while one was open for 16% of the time, Pallas kernels for 0%

commit v1 on v0

--- a/solution.py
+++ b/solution.py
@@ -1,6 +1,11 @@
+import functools
+
 import jax
 import jax.numpy as jnp
+import numpy as np
 from jax import lax
+from jax.experimental import pallas as pl
+from jax.experimental.pallas import tpu as pltpu
 from jax.sharding import PartitionSpec as P
 
 GROUPS = 32
@@ -219,6 +224,461 @@
     return (down, video_grad, conv_weight_grad, down_weight_grad)
 
 
+F32 = jnp.float32
+BF16 = jnp.bfloat16
+MESH = pl.DeviceIdType.MESH
+WIDE = 256
+OWN = 32
+
+
+def lane_swap():
+    lane = np.arange(512)
+    outer, inner, channel = lane // 128, lane // 32 % 4, lane % 32
+    table = np.zeros((512, 512), np.float32)
+    table[lane, inner * 128 + outer * 32 + channel] = 1.0
+    return jnp.asarray(table, BF16)
+
+
+def lane_gather():
+    lane = np.arange(1024)
+    owner, part, channel = lane // 128, lane // 32 % 4, lane % 32
+    table = np.zeros((4, 1024, 256), np.float32)
+    table[part, lane, owner * 32 + channel] = 1.0
+    return jnp.asarray(table, BF16)
+
+
+def column_pick():
+    table = np.zeros((2, 3, 256, 4, 4, 32), np.float32)
+    for core in range(2):
+        for tap in range(3):
+            for chip in range(4):
+                for channel in range(32):
+                    table[core, tap, 64 * chip + 32 * core + channel, chip, tap, channel] = 1.0
+    return jnp.asarray(table.reshape(2, 768, 512), BF16)
+
+
+def dot(lhs, rhs):
+    return jnp.dot(lhs, rhs, preferred_element_type=F32)
+
+
+def dot_nt(lhs, rhs):
+    return lax.dot_general(lhs, rhs, (((1,), (1,)), ((), ())), preferred_element_type=F32)
+
+
+def move_cols(block, distance):
+    if distance == 0:
+        return block
+    rows = block.shape[0]
+    col = lax.broadcasted_iota(jnp.int32, block.shape, 0) % 8 + distance
+    turned = pltpu.roll(block, (-distance) % rows, 0)
+    return jnp.where((col >= 0) & (col < 8), turned, 0.0)
+
+
+def fold_taps(result, outer, distances):
+    parts = result.reshape(outer, 4, 8, 128)
+    place = lax.broadcasted_iota(jnp.int32, (outer * 8, 128), 1) // OWN
+    total = None
+    for tap in range(3):
+        layer = jnp.zeros((outer * 8, 128), F32)
+        for clip in range(4):
+            block = parts[:, clip].reshape(outer * 8, 128)
+            turn = (OWN * (clip - tap)) % 128
+            if turn:
+                block = pltpu.roll(block, turn, 1)
+            layer = jnp.where(place == clip, block, layer)
+        layer = move_cols(layer, distances[tap])
+        total = layer if total is None else total + layer
+    return total
+
+
+def group_total(row):
+    first = lax.broadcasted_iota(jnp.int32, (128, 128), 0) // 8
+    second = lax.broadcasted_iota(jnp.int32, (128, 128), 1) // 8
+    same = (first == second).astype(F32)
+    wide = jnp.broadcast_to(row, (8, 128))
+    return jnp.dot(wide, same, preferred_element_type=F32, precision=lax.Precision.HIGHEST)[0:1]
+
+
+def block_kernel(
+    meta_ref, video_ref, cw_ref, dw_ref, og_ref, swap_ref, gather_ref, pick_ref,
+    down_ref, vgrad_ref, cgrad_ref, dgrad_ref,
+    meta_all, v_send, v_all, w_send, w_all, og_all, h_all, g_all, r_all, d_send, d_all,
+    x_send, x_all, h_full, g_full, r_full, og_up, rows_fwd, cells, normed_ref, mask_ref,
+    res_ref, stack_t, og_stack_t, back_ref, send_sems, recv_sems,
+):
+    chip = lax.axis_index("fsdp")
+    core = lax.axis_index("tile")
+    me = chip * 2 + core
+
+    def peer(index):
+        return {"fsdp": index // 2, "tile": index % 2}
+
+    barrier = pltpu.get_barrier_semaphore()
+    for step in range(1, 8):
+        pl.semaphore_signal(barrier, inc=1, device_id=peer((me + step) % 8), device_id_type=MESH)
+    pl.semaphore_wait(barrier, 7)
+
+    def send(phase, step, src, dst, to):
+        copy = pltpu.make_async_remote_copy(
+            src_ref=src, dst_ref=dst, send_sem=send_sems.at[phase, step],
+            recv_sem=recv_sems.at[phase, step], device_id=peer(to), device_id_type=MESH,
+        )
+        copy.start()
+        return copy
+
+    def send_all(phase, source, target):
+        return [send(phase, s, source((me + s) % 8), target, (me + s) % 8) for s in range(1, 8)]
+
+    def arrived(copies):
+        for copy in copies:
+            copy.wait_recv()
+
+    meta_all[chip] = meta_ref[...]
+    meta_copies = [
+        send(3, s, meta_ref, meta_all.at[chip], ((chip + s) % 4) * 2 + core) for s in range(1, 4)
+    ]
+    halves = []
+    for half in range(2):
+        halves.append(
+            jnp.concatenate(
+                [video_ref[64 * t : 64 * t + 64, 128 * half : 128 * half + 128] for t in range(4)],
+                axis=1,
+            )
+        )
+    packed = dot(jnp.concatenate(halves, axis=0), swap_ref[...]).astype(BF16)
+    for index in range(8):
+        half, quarter = index // 4, index % 4
+        v_send[index] = packed[64 * half : 64 * half + 64, 128 * quarter : 128 * quarter + 128]
+    v_copies = send_all(0, lambda to: v_send.at[to], v_all.at[me])
+    v_all[me] = v_send[me]
+    og_all[me] = og_ref[...]
+    og_copies = send_all(1, lambda to: og_ref, og_all.at[me])
+
+    picks = None
+    for tap in range(3):
+        rows = [cw_ref[:, (3 * ab + tap) * WIDE : (3 * ab + tap + 1) * WIDE] for ab in range(9)]
+        rows += [dw_ref[:, (3 * b + tap) * WIDE : (3 * b + tap + 1) * WIDE] for b in range(3)]
+        term = dot(jnp.concatenate(rows, axis=0), pick_ref[core, 256 * tap : 256 * tap + 256, :])
+        picks = term if picks is None else picks + term
+    for other in range(4):
+        w_send[other] = picks[:, 128 * other : 128 * other + 128].astype(BF16)
+    w_all[chip] = w_send[chip]
+    w_copies = []
+    for s in range(1, 4):
+        to = (chip + s) % 4
+        w_copies.append(send(2, s, w_send.at[to], w_all.at[chip], to * 2 + core))
+
+    mine = pl.ds(pl.multiple_of(core * OWN, OWN), OWN)
+    for ab in range(9):
+        for tap in range(3):
+            at = (3 * ab + tap) * WIDE
+            rows_fwd[ab, 32 * tap : 32 * tap + 32, :] = cw_ref[mine, at : at + WIDE]
+        rows_fwd[ab, 96:128, :] = jnp.zeros((32, WIDE), BF16)
+    for b in range(3):
+        for tap in range(3):
+            at = (3 * b + tap) * WIDE
+            rows_fwd[9 + b, 32 * tap : 32 * tap + 32, :] = dw_ref[mine, at : at + WIDE]
+        rows_fwd[9 + b, 96:128, :] = jnp.zeros((32, WIDE), BF16)
+
+    edge = jnp.zeros((10, 32, WIDE), BF16)
+    for t in range(2):
+        h_full[t] = edge
+        g_full[8 + t] = edge
+    for t in range(8):
+        for full, off in ((h_full, 2), (g_full, 0)):
+            full[t + off, 0] = jnp.zeros((32, WIDE), BF16)
+            full[t + off, 9] = jnp.zeros((32, WIDE), BF16)
+        r_full[t, 4, 0] = jnp.zeros((32, WIDE), BF16)
+
+    arrived(meta_copies)
+    place1 = lax.broadcasted_iota(jnp.int32, (1, 128), 1) // OWN
+    start = jnp.zeros((1, 128), F32)
+    high = jnp.zeros((1, 128), F32)
+    width = jnp.zeros((1, 128), F32)
+    for clip in range(4):
+        start = jnp.where(place1 == clip, meta_all[clip, 0:1, :], start)
+        high = jnp.where(place1 == clip, meta_all[clip, 1:2, :], high)
+        width = jnp.where(place1 == clip, meta_all[clip, 2:3, :], width)
+    count = (8.0 - start) * high * width * 8.0
+    row_id = lax.broadcasted_iota(jnp.int32, (512, 128), 0)
+    in_time = (row_id // 64).astype(F32) >= start
+    in_rows = (row_id // 8 % 8).astype(F32) < high
+    in_cols = (row_id % 8).astype(F32) < width
+    mask_ref[...] = jnp.where(in_time & in_rows & in_cols, 1.0, 0.0)
+
+    arrived(v_copies)
+    stacked = jnp.concatenate(
+        [
+            jnp.concatenate([v_all[2 * other + c] for other in range(4)], axis=1)
+            for c in range(2)
+        ],
+        axis=0,
+    )
+    unpacked = dot(stacked, swap_ref[...])
+    for t in range(8):
+        c, q = t // 4, t % 4
+        cells[64 * t : 64 * t + 64, :] = unpacked[64 * c : 64 * c + 64, 128 * q : 128 * q + 128]
+    mask = mask_ref[...]
+    centre = group_total(jnp.sum(mask * cells[...], axis=0, keepdims=True)) / count
+    offset = cells[...] - centre
+    spread = group_total(jnp.sum(mask * offset * offset, axis=0, keepdims=True)) / count
+    inverse = lax.rsqrt(spread + EPSILON)
+    normed = offset * inverse
+    normed_ref[...] = normed
+    h_all[me] = (mask * (normed / (1.0 + jnp.exp(-normed)))).astype(BF16)
+    h_copies = send_all(4, lambda to: h_all.at[me], h_all.at[me])
+
+    arrived(og_copies)
+    up_row = lax.broadcasted_iota(jnp.int32, (128, 64), 0)
+    up_col = lax.broadcasted_iota(jnp.int32, (128, 64), 1)
+    lift = ((up_row // 8 == up_col // 4) & (up_row % 8 == 2 * (up_col % 4))).astype(F32).astype(BF16)
+    for c in range(2):
+        raised = [dot(lift, og_all[2 * clip + c]).reshape(16, 8, WIDE) for clip in range(4)]
+        og_up[4 * c : 4 * c + 4] = (
+            jnp.concatenate(raised, axis=1).astype(BF16).reshape(4, 4, 32, WIDE)
+        )
+    arrived(w_copies)
+
+    def res_grad_frame(t, carry):
+        lhs = og_up[t].reshape(128, WIDE)
+        layers = []
+        for b in range(3):
+            panel = w_all[:, 64 * (9 + b) : 64 * (10 + b), :].reshape(256, 128)
+            layers.append(fold_taps(dot(lhs, panel), 4, (0, -1, -2)).reshape(4, 8, 128))
+        even = layers[0] + jnp.concatenate([jnp.zeros((1, 8, 128), F32), layers[2][:3]], axis=0)
+        both = jnp.stack([even, layers[1]], axis=1).reshape(64, 128)
+        at = pl.ds(pl.multiple_of(64 * t, 64), 64)
+        value = (mask_ref[at, :] * both).astype(BF16)
+        g_all[me, at, :] = value
+        wide = value.astype(F32)
+        res_ref[at, :] = wide
+        shifts = [move_cols(wide, 1 - tap) for tap in range(3)]
+        place = lax.broadcasted_iota(jnp.int32, (64, 128), 1) // OWN
+        split = []
+        for clip in range(4):
+            block = jnp.zeros((64, 128), F32)
+            for tap in range(3):
+                turn = (OWN * (tap - clip)) % 128
+                moved = pltpu.roll(shifts[tap], turn, 1) if turn else shifts[tap]
+                block = jnp.where(place == tap, moved, block)
+            split.append(block.reshape(8, 8, 128))
+        rows = jnp.concatenate(split, axis=1).reshape(256, 128)
+        stack_t[t] = rows.T.astype(BF16)
+        return carry
+
+    lax.fori_loop(0, 8, res_grad_frame, 0)
+    g_copies = send_all(5, lambda to: g_all.at[me], g_all.at[me])
+
+    def og_frame(t, carry):
+        lhs = og_up[t].reshape(128, WIDE)
+        from_row = lax.broadcasted_iota(jnp.int32, (WIDE, 128), 0)
+        to_lane = lax.broadcasted_iota(jnp.int32, (WIDE, 128), 1)
+        total = None
+        for tap in range(3):
+            chosen = (to_lane // OWN == tap) & (from_row == to_lane % OWN + OWN * me)
+            term = move_cols(dot(lhs, chosen.astype(F32).astype(BF16)), -tap)
+            total = term if total is None else total + term
+        og_stack_t[t] = total.T.astype(BF16)
+        return carry
+
+    lax.fori_loop(0, 8, og_frame, 0)
+
+    def assemble(source, t):
+        at = pl.ds(pl.multiple_of(128 * t, 128), 128)
+        lhs = jnp.concatenate([source[d, at, :] for d in range(8)], axis=1)
+        blocks = [dot(lhs, gather_ref[clip]).reshape(16, 8, WIDE) for clip in range(4)]
+        return jnp.concatenate(blocks, axis=1).astype(BF16).reshape(2, 8, 32, WIDE)
+
+    arrived(h_copies)
+
+    def fill_hidden(t, carry):
+        h_full[pl.ds(2 * t + 2, 2), 1:9] = assemble(h_all, t)
+        return carry
+
+    lax.fori_loop(0, 4, fill_hidden, 0)
+
+    def conv_frame(t, carry):
+        total = None
+        for a in range(3):
+            for b in range(3):
+                window = h_full[t + a, b : b + 8].reshape(256, WIDE)
+                term = dot_nt(window, rows_fwd[3 * a + b])
+                total = term if total is None else total + term
+        folded = fold_taps(total, 8, (-1, 0, 1))
+        at = pl.ds(pl.multiple_of(64 * t, 64), 64)
+        r_all[me, at, :] = (mask_ref[at, :] * (cells[at, :] + folded)).astype(BF16)
+        return carry
+
+    lax.fori_loop(0, 8, conv_frame, 0)
+    r_copies = send_all(6, lambda to: r_all.at[me], r_all.at[me])
+
+    arrived(g_copies)
+
+    def fill_grad(t, carry):
+        g_full[pl.ds(2 * t, 2), 1:9] = assemble(g_all, t)
+        return carry
+
+    lax.fori_loop(0, 4, fill_grad, 0)
+
+    def back_frame(t, carry):
+        total = None
+        for a in range(3):
+            for b in range(3):
+                window = g_full[t + 2 - a, 2 - b : 10 - b].reshape(256, WIDE)
+                at = 64 * (3 * a + b)
+                term = dot(window, w_all[:, at : at + 64, :].reshape(256, 128))
+                total = term if total is None else total + term
+        at = pl.ds(pl.multiple_of(64 * t, 64), 64)
+        back_ref[at, :] = fold_taps(total, 8, (1, 0, -1))
+        return carry
+
+    lax.fori_loop(0, 8, back_frame, 0)
+    mask = mask_ref[...]
+    normed = normed_ref[...]
+    gate = 1.0 / (1.0 + jnp.exp(-normed))
+    pushed = mask * back_ref[...] * gate * (1.0 + normed * (1.0 - gate))
+    mean_push = group_total(jnp.sum(pushed, axis=0, keepdims=True)) / count
+    mean_pair = group_total(jnp.sum(pushed * normed, axis=0, keepdims=True)) / count
+    through = inverse * (pushed - mean_push - normed * mean_pair)
+    back_ref[...] = mask * through + res_ref[...]
+    for c in range(2):
+        quarter = [back_ref[64 * (4 * c + q) : 64 * (4 * c + q) + 64, :] for q in range(4)]
+        swapped = dot(jnp.concatenate(quarter, axis=1).astype(BF16), swap_ref[...]).astype(BF16)
+        for other in range(4):
+            x_send[2 * other + c] = swapped[:, 128 * other : 128 * other + 128]
+    x_all[me] = x_send[me]
+    x_copies = send_all(8, lambda to: x_send.at[to], x_all.at[me])
+
+    lhs = jnp.concatenate([stack_t[t] for t in range(8)], axis=1)
+    for a in range(3):
+        for b in range(3):
+            rhs = h_full[a : a + 8, b : b + 8].reshape(2048, WIDE)
+            grad = dot(lhs, rhs)
+            for tap in range(3):
+                at = (9 * a + 3 * b + tap) * WIDE
+                cgrad_ref[mine, at : at + WIDE] = grad[32 * tap : 32 * tap + 32]
+    sibling = chip * 2 + (1 - core)
+    c_copy = send(9, 0, cgrad_ref.at[mine], cgrad_ref.at[mine], sibling)
+
+    arrived(r_copies)
+
+    def fill_residual(t, carry):
+        r_full[pl.ds(2 * t, 2), 0:4] = assemble(r_all, t).reshape(2, 4, 2, 32, WIDE)
+        return carry
+
+    lax.fori_loop(0, 4, fill_residual, 0)
+
+    def down_frame(t, carry):
+        total = None
+        for b in range(3):
+            window = r_full[t, b // 2 : b // 2 + 4, b % 2].reshape(128, WIDE)
+            term = dot_nt(window, rows_fwd[9 + b])
+            total = term if total is None else total + term
+        folded = fold_taps(total, 4, (0, 1, 2)).astype(BF16)
+        to_row = lax.broadcasted_iota(jnp.int32, (16, 32), 0)
+        from_row = lax.broadcasted_iota(jnp.int32, (16, 32), 1)
+        even = (from_row == to_row * 2).astype(F32).astype(BF16)
+        d_send[t] = dot(even, folded).astype(BF16)
+        return carry
+
+    lax.fori_loop(0, 8, down_frame, 0)
+
+    def frames_of(to):
+        return pl.ds(4 * (to % 2), 4)
+
+    d_all[me] = d_send[frames_of(me)]
+    d_copies = send_all(7, lambda to: d_send.at[frames_of(to)], d_all.at[me])
+    lhs = jnp.concatenate([og_stack_t[t] for t in range(8)], axis=1)
+    for b in range(3):
+        rhs = r_full[:, b // 2 : b // 2 + 4, b % 2].reshape(1024, WIDE)
+        grad = dot(lhs, rhs)
+        for tap in range(3):
+            at = (3 * b + tap) * WIDE
+            dgrad_ref[mine, at : at + WIDE] = grad[32 * tap : 32 * tap + 32]
+    g_copy = send(9, 1, dgrad_ref.at[mine], dgrad_ref.at[mine], sibling)
+
+    arrived(x_copies)
+    lhs = jnp.concatenate([x_all[d] for d in range(8)], axis=1)
+    for t in range(4):
+        vgrad_ref[64 * t : 64 * t + 64, :] = dot(lhs, gather_ref[t]).astype(BF16)
+    arrived(d_copies)
+    lhs = jnp.concatenate([d_all[d].reshape(64, 128) for d in range(8)], axis=1)
+    down_ref[...] = dot(lhs, gather_ref[chip]).astype(BF16)
+    arrived([c_copy, g_copy])
+    for copies in (
+        meta_copies, v_copies, og_copies, w_copies, h_copies, g_copies, r_copies, x_copies,
+        d_copies, [c_copy, g_copy],
+    ):
+        for copy in copies:
+            copy.wait_send()
+
+
+def fused(video, conv_weight, down_weight, out_grad, clip_bucket, start_frame, bucket_res):
+    bucket_ids = jnp.arange(bucket_res.shape[0], dtype=jnp.int32)
+    picked = (clip_bucket[:, None] == bucket_ids[None, :]).astype(jnp.int32)
+    limits = jnp.sum(picked[:, :, None] * bucket_res[None, :, :], axis=1)
+    facts = jnp.concatenate([start_frame, limits[0], jnp.zeros((5,), jnp.int32)]).astype(F32)
+    meta = jnp.broadcast_to(facts[:, None], (8, 128))
+    vmem = pl.BlockSpec(memory_space=pltpu.VMEM)
+    full = pltpu.VMEM((10, 10, 32, WIDE), BF16)
+    gathered = pltpu.VMEM((8, 512, 128), BF16)
+    wide = pltpu.VMEM((512, 128), F32)
+    piece = pltpu.VMEM((8, 64, 128), BF16)
+    down, video_grad, conv_grad, down_grad = pl.pallas_call(
+        block_kernel,
+        out_shape=(
+            jax.ShapeDtypeStruct((64, WIDE), BF16),
+            jax.ShapeDtypeStruct((256, WIDE), BF16),
+            jax.ShapeDtypeStruct(conv_weight.shape, F32),
+            jax.ShapeDtypeStruct(down_weight.shape, F32),
+        ),
+        in_specs=[vmem] * 8,
+        out_specs=(vmem,) * 4,
+        scratch_shapes=[
+            pltpu.VMEM((4, 8, 128), F32),
+            piece,
+            piece,
+            pltpu.VMEM((4, 768, 128), BF16),
+            pltpu.VMEM((4, 768, 128), BF16),
+            pltpu.VMEM((8, 64, WIDE), BF16),
+            gathered,
+            gathered,
+            gathered,
+            pltpu.VMEM((8, 16, 128), BF16),
+            pltpu.VMEM((8, 4, 16, 128), BF16),
+            piece,
+            piece,
+            full,
+            full,
+            pltpu.VMEM((8, 5, 2, 32, WIDE), BF16),
+            pltpu.VMEM((8, 4, 32, WIDE), BF16),
+            pltpu.VMEM((12, 128, WIDE), BF16),
+            wide,
+            wide,
+            wide,
+            wide,
+            pltpu.VMEM((8, 128, 256), BF16),
+            pltpu.VMEM((8, 128, 128), BF16),
+            wide,
+            pltpu.SemaphoreType.DMA((10, 8)),
+            pltpu.SemaphoreType.DMA((10, 8)),
+        ],
+        compiler_params=pltpu.CompilerParams(
+            collective_id=0, has_side_effects=True, vmem_limit_bytes=50 * 2**20
+        ),
+    )(
+        meta,
+        video.reshape(256, WIDE),
+        conv_weight,
+        down_weight,
+        out_grad.reshape(64, WIDE),
+        lane_swap(),
+        lane_gather(),
+        column_pick(),
+    )
+    return (down.reshape(out_grad.shape), video_grad.reshape(video.shape), conv_grad, down_grad)
+
+
 def solution(mesh):
     placed = (
         P(("mix", "fsdp"), "tile", None, None, None),
@@ -230,7 +690,7 @@
         P(),
     )
     return jax.shard_map(
-        shards,
+        fused if mesh.shape["tile"] == 2 and mesh.shape["fsdp"] == 4 else shards,
         mesh=mesh,
         in_specs=placed,
         out_specs=(

time: 258 us -> 79.5 us (0.31)
  waiting for transfers between devices: 153 us -> 0 us
  Pallas kernels: 0 us -> 66.4 us
  local copies, waits for them, and re-layouts: 38.5 us -> 9.81 us
  other arithmetic: 18.7 us -> 0.88 us
  between operations: 17.6 us -> 1.95 us
  matrix products: 15.4 us -> 0 us
  blocking collectives: 10.9 us -> 0 us
  starting transfers between devices: 3.55 us -> 0 us
    reduce_scatter x2 -> x0, waiting for transfers between devices: 96.6 us -> none  [the longest x1 51.5 us: shards(): lax.psum_scatter(conv_term, ('fsdp', 'tile'), scatter_dimension=0, tiled=...]
    pallas_call x0 -> x1, Pallas kernels: none -> 66.4 us  [fused(): pl.pallas_call(block_kernel, out_shape=(jax.ShapeDtypeStruct((64, WIDE),...]
    all_gather x3 -> x0, waiting for transfers between devices: 53.7 us -> none  [the longest x1 22.8 us: shards(): weight_panel = lax.all_gather(down_weight, 'fsdp', axis=0, tiled=True)]
    dot_general x12 -> x0, matrix products: 15.4 us -> none  [the longest x3 5.77 us: transpose_conv(): lax.dot_general(group, panel[:, 9 * tap_time:9 * tap_time + 9, :], (((0,...]
    scatter-add x9 -> x0, other arithmetic: 11.9 us -> none  [shards(): spread_back = spread_back.at[:, :, tap_row:tap_row + side_cells:2, tap_co...]
    reshape x4 -> x2, local copies, waits for them, and re-layouts: 11.2 us -> 1.4 us  [the longest x1 0.78 us: fused(): out_grad.reshape(64, WIDE)]
    psum x3 -> x0, blocking collectives: 8.5 us -> none  [the longest x1 3.44 us: shards(): lax.psum(jnp.sum(cell_weight * offset * offset, axis=summed_axes), 'tile')]
    all_gather x2 -> x0, local copies, waits for them, and re-layouts: 7.55 us -> none  [the longest x1 5.98 us: shards(): lax.all_gather(conv_weight, 'fsdp', axis=0, tiled=True)]
  transfers between devices with their start and end apart: 7 -> 0, of which waited for: 6 -> 0; matrix products, arithmetic and copies ran while one was open for 16% -> 0% of each run, Pallas kernels for 0% -> 0%
where the time goes in v1:
time: 79.5 us; the launch traced here: 79.1 us
  Pallas kernels  66.4 us (84%)
  local copies, waits for them, and re-layouts  9.81 us (12%)
  between operations  1.95 us (2%)
  other arithmetic  0.88 us (1%)
    pallas_call x1, Pallas kernels, fused(): pl.pallas_call(block_kernel, out_shape=(jax.ShapeDtypeStruct((64, WIDE),...  66.4 us
    unnamed x11, local copies, waits for them, and re-layouts  8.33 us

profile of v1, /device:TPU:0, one launch (start us, length us, event | category | flops | bytes accessed | tf_op | source)
XLA Modules:
  0.0 79.1 jit_solution(6392226450877560261)
XLA Ops:
  1.9 0.8 %multiply_reduce_fusion = s32[2]{0:T(128)S(1)} fusion(s32[4,2]{0,1:T(2,128)} %param.16, s32[4]{0:T(128)S(1)} %compare_convert_fusion), kind=kLoop, calls=%fused_computation.1 | loop fusion | flops 14 | bytes 56 | tf_op jit(solution)/shard_map/reduce_sum | solution.py:619
  2.7 0.1 add_convert_fusion
  2.8 0.1 broadcast_in_dim.2.meta_ref
  2.9 0.8 reshape.57.og_ref
  3.7 0.0 copy-start
  3.7 1.2 %copy-done = bf16[64,6912]{1,0:T(8,128)(2,1)S(1)} copy-done((bf16[64,6912]{1,0:T(8,128)(2,1)S(1)}, bf16[64,6912]{1,0:T(8,128)(2,1)}, u32[]{:S(2)}) %copy-start) | copy-done | bytes 884760
  4.8 0.0 copy-start.1
  4.8 1.0 %copy-done.1 = bf16[512,512]{1,0:T(8,128)(2,1)S(1)} copy-done((bf16[512,512]{1,0:T(8,128)(2,1)S(1)}, bf16[512,512]{1,0:T(8,128)(2,1)}, u32[]{:S(2)}) %copy-start.1) | copy-done | bytes 524312
  5.9 0.0 copy-start.2
  5.9 1.0 %copy-done.2 = bf16[64,2304]{1,0:T(8,128)(2,1)S(1)} copy-done((bf16[64,2304]{1,0:T(8,128)(2,1)S(1)}, bf16[64,2304]{1,0:T(8,128)(2,1)}, u32[]{:S(2)}) %copy-start.2) | copy-done | bytes 294936
  6.8 0.0 copy-start.3
  6.8 0.9 %copy-done.3 = bf16[1,4,8,8,256]{4,3,2,1,0:T(8,128)(2,1)S(1)} copy-done((bf16[1,4,8,8,256]{4,3,2,1,0:T(8,128)(2,1)S(1)}, bf16[1,4,8,8,256]{4,3,2,1,0:T(8,128)(2,1)}, u32[]{:S(2)}) %copy-start.3) | copy-done | bytes 131096
  7.7 66.4 %shard_map.129 = (bf16[64,256]{1,0:T(8,128)(2,1)S(1)}, bf16[256,256]{1,0:T(8,128)(2,1)S(1)}, f32[64,6912]{1,0:T(8,128)}, f32[64,2304]{1,0:T(8,128)S(1)}) custom-call(f32[8,128]{1,0:T(8,128)S(1)} %broadcast_in_dim.2.meta_ref, bf16[256,256]{1,0:T(8,128)(2,1)S(1)} %bitcast.4, bf16[64,6912]{1,0:T(8,128)(2,1)S(1)} %copy-done, bf16[64,2304]{1,0:T(8,128)(2,1)S(1)} %copy-done.2, ...), custom_call_target="tpu_custom_call" | custom-call | tf_op jit(solution)/shard_map/pallas_call | solution.py:627
  74.2 0.6 reshape.58
  74.8 0.7 copy.19
  75.5 2.8 %copy.20 = f32[64,6912]{1,0:T(8,128)} copy(f32[64,6912]{1,0:T(8,128)} %get-tuple-element.18) | data formatting | bytes 3538944
  78.3 0.8 %copy.21 = f32[64,2304]{1,0:T(8,128)} copy(f32[64,2304]{1,0:T(8,128)S(1)} %get-tuple-element.19) | data formatting | bytes 1179648
  (2 shorter events, 0.0 us)
Async XLA Ops:
  3.7 1.2 %copy-start = (bf16[64,6912]{1,0:T(8,128)(2,1)S(1)}, bf16[64,6912]{1,0:T(8,128)(2,1)}, u32[]{:S(2)}) copy-start(bf16[64,6912]{1,0:T(8,128)(2,1)} %cw_ref.1) | copy-start | bytes 2654212
  4.8 1.0 %copy-start.1 = (bf16[512,512]{1,0:T(8,128)(2,1)S(1)}, bf16[512,512]{1,0:T(8,128)(2,1)}, u32[]{:S(2)}) copy-start(bf16[512,512]{1,0:T(8,128)(2,1)} %constant.3.clone.swap_ref) | copy-start | bytes 1572868
  5.9 1.0 %copy-start.2 = (bf16[64,2304]{1,0:T(8,128)(2,1)S(1)}, bf16[64,2304]{1,0:T(8,128)(2,1)}, u32[]{:S(2)}) copy-start(bf16[64,2304]{1,0:T(8,128)(2,1)} %dw_ref.1) | copy-start | bytes 884740
  6.8 0.9 %copy-start.3 = (bf16[1,4,8,8,256]{4,3,2,1,0:T(8,128)(2,1)S(1)}, bf16[1,4,8,8,256]{4,3,2,1,0:T(8,128)(2,1)}, u32[]{:S(2)}) copy-start(bf16[1,4,8,8,256]{4,3,2,1,0:T(8,128)(2,1)} %param.10) | copy-start | bytes 393220

commit v2 on v1

--- a/solution.py
+++ b/solution.py
@@ -300,18 +300,34 @@
 
 
 def block_kernel(
-    meta_ref, video_ref, cw_ref, dw_ref, og_ref, swap_ref, gather_ref, pick_ref,
+    bucket_ref, start_ref, res_table_ref, video_ref, cw_hbm, dw_hbm, og_ref, swap_hbm,
+    gather_hbm, pick_hbm,
     down_ref, vgrad_ref, cgrad_ref, dgrad_ref,
+    meta_ref, cw_ref, dw_ref, swap_ref, gather_ref, pick_ref,
     meta_all, v_send, v_all, w_send, w_all, og_all, h_all, g_all, r_all, d_send, d_all,
     x_send, x_all, h_full, g_full, r_full, og_up, rows_fwd, cells, normed_ref, mask_ref,
-    res_ref, stack_t, og_stack_t, back_ref, send_sems, recv_sems,
+    res_ref, stack_t, og_stack_t, back_ref, load_sems, send_sems, recv_sems,
 ):
     chip = lax.axis_index("fsdp")
     core = lax.axis_index("tile")
     me = chip * 2 + core
+    sibling = chip * 2 + (1 - core)
 
     def peer(index):
         return {"fsdp": index // 2, "tile": index % 2}
+
+    loads = {}
+    for index, (name, source, target) in enumerate(
+        (
+            ("swap", swap_hbm, swap_ref),
+            ("dw", dw_hbm, dw_ref),
+            ("pick", pick_hbm.at[core], pick_ref),
+            ("cw", cw_hbm, cw_ref),
+            ("gather", gather_hbm, gather_ref),
+        )
+    ):
+        loads[name] = pltpu.make_async_copy(source, target, load_sems.at[index])
+        loads[name].start()
 
     barrier = pltpu.get_barrier_semaphore()
     for step in range(1, 8):
@@ -329,14 +345,42 @@
     def send_all(phase, source, target):
         return [send(phase, s, source((me + s) % 8), target, (me + s) % 8) for s in range(1, 8)]
 
+    def spread_out(phase, target):
+        copies = [send(phase, 4, target.at[me], target.at[me], sibling)]
+        for s in range(1, 4):
+            copies.append(send(phase, s, target.at[me], target.at[me], ((chip + s) % 4) * 2 + core))
+        return copies
+
+    def relay(phase, target, copies):
+        passed = []
+        for s in range(1, 4):
+            copies[s].wait_recv()
+            slot = ((chip + 4 - s) % 4) * 2 + core
+            passed.append(send(phase, 4 + s, target.at[slot], target.at[slot], sibling))
+        copies.extend(passed)
+
+    def complete(copies):
+        copies[0].wait_recv()
+        for copy in copies[4:]:
+            copy.wait_recv()
+
     def arrived(copies):
         for copy in copies:
             copy.wait_recv()
 
-    meta_all[chip] = meta_ref[...]
+    bucket = bucket_ref[0]
+    high, width = jnp.int32(0), jnp.int32(0)
+    for index in range(res_table_ref.shape[0]):
+        high = high + jnp.where(bucket == index, res_table_ref[index, 0], 0)
+        width = width + jnp.where(bucket == index, res_table_ref[index, 1], 0)
+    line = lax.broadcasted_iota(jnp.int32, (8, 128), 0)
+    facts = jnp.where(line == 0, start_ref[0], jnp.where(line == 1, high, width)).astype(F32)
+    meta_ref[...] = facts
+    meta_all[chip] = facts
     meta_copies = [
         send(3, s, meta_ref, meta_all.at[chip], ((chip + s) % 4) * 2 + core) for s in range(1, 4)
     ]
+    loads["swap"].wait()
     halves = []
     for half in range(2):
         halves.append(
@@ -351,44 +395,32 @@
         v_send[index] = packed[64 * half : 64 * half + 64, 128 * quarter : 128 * quarter + 128]
     v_copies = send_all(0, lambda to: v_send.at[to], v_all.at[me])
     v_all[me] = v_send[me]
-    og_all[me] = og_ref[...]
-    og_copies = send_all(1, lambda to: og_ref, og_all.at[me])
-
-    picks = None
-    for tap in range(3):
-        rows = [cw_ref[:, (3 * ab + tap) * WIDE : (3 * ab + tap + 1) * WIDE] for ab in range(9)]
-        rows += [dw_ref[:, (3 * b + tap) * WIDE : (3 * b + tap + 1) * WIDE] for b in range(3)]
-        term = dot(jnp.concatenate(rows, axis=0), pick_ref[core, 256 * tap : 256 * tap + 256, :])
-        picks = term if picks is None else picks + term
-    for other in range(4):
-        w_send[other] = picks[:, 128 * other : 128 * other + 128].astype(BF16)
-    w_all[chip] = w_send[chip]
-    w_copies = []
-    for s in range(1, 4):
-        to = (chip + s) % 4
-        w_copies.append(send(2, s, w_send.at[to], w_all.at[chip], to * 2 + core))
-
-    mine = pl.ds(pl.multiple_of(core * OWN, OWN), OWN)
-    for ab in range(9):
+    og_all[me] = og_ref[0].astype(F32).reshape(64, WIDE).astype(BF16)
+    og_copies = spread_out(1, og_all)
+
+    loads["dw"].wait()
+    loads["pick"].wait()
+
+    def exchange_columns(phase, ref, blocks, first):
+        picks = None
         for tap in range(3):
-            at = (3 * ab + tap) * WIDE
-            rows_fwd[ab, 32 * tap : 32 * tap + 32, :] = cw_ref[mine, at : at + WIDE]
-        rows_fwd[ab, 96:128, :] = jnp.zeros((32, WIDE), BF16)
-    for b in range(3):
-        for tap in range(3):
-            at = (3 * b + tap) * WIDE
-            rows_fwd[9 + b, 32 * tap : 32 * tap + 32, :] = dw_ref[mine, at : at + WIDE]
-        rows_fwd[9 + b, 96:128, :] = jnp.zeros((32, WIDE), BF16)
-
-    edge = jnp.zeros((10, 32, WIDE), BF16)
-    for t in range(2):
-        h_full[t] = edge
-        g_full[8 + t] = edge
-    for t in range(8):
-        for full, off in ((h_full, 2), (g_full, 0)):
-            full[t + off, 0] = jnp.zeros((32, WIDE), BF16)
-            full[t + off, 9] = jnp.zeros((32, WIDE), BF16)
-        r_full[t, 4, 0] = jnp.zeros((32, WIDE), BF16)
+            at = [(3 * block + tap) * WIDE for block in range(blocks)]
+            rows = jnp.concatenate([ref[:, low : low + WIDE] for low in at], axis=0)
+            term = dot(rows, pick_ref[256 * tap : 256 * tap + 256, :])
+            picks = term if picks is None else picks + term
+        part = pl.ds(first, 64 * blocks)
+        for other in range(4):
+            w_send[other, part, :] = picks[:, 128 * other : 128 * other + 128].astype(BF16)
+        w_all[chip, part, :] = w_send[chip, part, :]
+        copies = []
+        for s in range(1, 4):
+            to = (chip + s) % 4
+            copies.append(
+                send(phase, s, w_send.at[to, part], w_all.at[chip, part], to * 2 + core)
+            )
+        return copies
+
+    dw_copies = exchange_columns(2, dw_ref, 3, 576)
 
     arrived(meta_copies)
     place1 = lax.broadcasted_iota(jnp.int32, (1, 128), 1) // OWN
@@ -426,9 +458,10 @@
     normed = offset * inverse
     normed_ref[...] = normed
     h_all[me] = (mask * (normed / (1.0 + jnp.exp(-normed)))).astype(BF16)
-    h_copies = send_all(4, lambda to: h_all.at[me], h_all.at[me])
-
-    arrived(og_copies)
+    h_copies = spread_out(4, h_all)
+
+    relay(1, og_all, og_copies)
+    complete(og_copies)
     up_row = lax.broadcasted_iota(jnp.int32, (128, 64), 0)
     up_col = lax.broadcasted_iota(jnp.int32, (128, 64), 1)
     lift = ((up_row // 8 == up_col // 4) & (up_row % 8 == 2 * (up_col % 4))).astype(F32).astype(BF16)
@@ -437,7 +470,7 @@
         og_up[4 * c : 4 * c + 4] = (
             jnp.concatenate(raised, axis=1).astype(BF16).reshape(4, 4, 32, WIDE)
         )
-    arrived(w_copies)
+    arrived(dw_copies)
 
     def res_grad_frame(t, carry):
         lhs = og_up[t].reshape(128, WIDE)
@@ -452,6 +485,39 @@
         g_all[me, at, :] = value
         wide = value.astype(F32)
         res_ref[at, :] = wide
+        return carry
+
+    lax.fori_loop(0, 8, res_grad_frame, 0)
+    g_copies = spread_out(5, g_all)
+
+    loads["cw"].wait()
+    cw_copies = exchange_columns(10, cw_ref, 9, 0)
+
+    mine = pl.ds(pl.multiple_of(core * OWN, OWN), OWN)
+    for ab in range(9):
+        for tap in range(3):
+            at = (3 * ab + tap) * WIDE
+            rows_fwd[ab, 32 * tap : 32 * tap + 32, :] = cw_ref[mine, at : at + WIDE]
+        rows_fwd[ab, 96:128, :] = jnp.zeros((32, WIDE), BF16)
+    for b in range(3):
+        for tap in range(3):
+            at = (3 * b + tap) * WIDE
+            rows_fwd[9 + b, 32 * tap : 32 * tap + 32, :] = dw_ref[mine, at : at + WIDE]
+        rows_fwd[9 + b, 96:128, :] = jnp.zeros((32, WIDE), BF16)
+
+    edge = jnp.zeros((10, 32, WIDE), BF16)
+    for t in range(2):
+        h_full[t] = edge
+        g_full[8 + t] = edge
+    for t in range(8):
+        for full, off in ((h_full, 2), (g_full, 0)):
+            full[t + off, 0] = jnp.zeros((32, WIDE), BF16)
+            full[t + off, 9] = jnp.zeros((32, WIDE), BF16)
+        r_full[t, 4, 0] = jnp.zeros((32, WIDE), BF16)
+
+    def stack_frame(t, carry):
+        at = pl.ds(pl.multiple_of(64 * t, 64), 64)
+        wide = res_ref[at, :]
         shifts = [move_cols(wide, 1 - tap) for tap in range(3)]
         place = lax.broadcasted_iota(jnp.int32, (64, 128), 1) // OWN
         split = []
@@ -466,8 +532,7 @@
         stack_t[t] = rows.T.astype(BF16)
         return carry
 
-    lax.fori_loop(0, 8, res_grad_frame, 0)
-    g_copies = send_all(5, lambda to: g_all.at[me], g_all.at[me])
+    lax.fori_loop(0, 8, stack_frame, 0)
 
     def og_frame(t, carry):
         lhs = og_up[t].reshape(128, WIDE)
@@ -489,7 +554,9 @@
         blocks = [dot(lhs, gather_ref[clip]).reshape(16, 8, WIDE) for clip in range(4)]
         return jnp.concatenate(blocks, axis=1).astype(BF16).reshape(2, 8, 32, WIDE)
 
-    arrived(h_copies)
+    relay(4, h_all, h_copies)
+    loads["gather"].wait()
+    complete(h_copies)
 
     def fill_hidden(t, carry):
         h_full[pl.ds(2 * t + 2, 2), 1:9] = assemble(h_all, t)
@@ -509,16 +576,20 @@
         r_all[me, at, :] = (mask_ref[at, :] * (cells[at, :] + folded)).astype(BF16)
         return carry
 
-    lax.fori_loop(0, 8, conv_frame, 0)
-    r_copies = send_all(6, lambda to: r_all.at[me], r_all.at[me])
-
-    arrived(g_copies)
+    lax.fori_loop(0, 4, conv_frame, 0)
+    relay(5, g_all, g_copies)
+    lax.fori_loop(4, 8, conv_frame, 0)
+    r_copies = spread_out(6, r_all)
+
+    complete(g_copies)
 
     def fill_grad(t, carry):
         g_full[pl.ds(2 * t, 2), 1:9] = assemble(g_all, t)
         return carry
 
     lax.fori_loop(0, 4, fill_grad, 0)
+
+    arrived(cw_copies)
 
     def back_frame(t, carry):
         total = None
@@ -549,6 +620,7 @@
     x_all[me] = x_send[me]
     x_copies = send_all(8, lambda to: x_send.at[to], x_all.at[me])
 
+    relay(6, r_all, r_copies)
     lhs = jnp.concatenate([stack_t[t] for t in range(8)], axis=1)
     for a in range(3):
         for b in range(3):
@@ -557,10 +629,9 @@
             for tap in range(3):
                 at = (9 * a + 3 * b + tap) * WIDE
                 cgrad_ref[mine, at : at + WIDE] = grad[32 * tap : 32 * tap + 32]
-    sibling = chip * 2 + (1 - core)
     c_copy = send(9, 0, cgrad_ref.at[mine], cgrad_ref.at[mine], sibling)
 
-    arrived(r_copies)
+    complete(r_copies)
 
     def fill_residual(t, carry):
         r_full[pl.ds(2 * t, 2), 0:4] = assemble(r_all, t).reshape(2, 4, 2, 32, WIDE)
@@ -603,10 +674,10 @@
         vgrad_ref[64 * t : 64 * t + 64, :] = dot(lhs, gather_ref[t]).astype(BF16)
     arrived(d_copies)
     lhs = jnp.concatenate([d_all[d].reshape(64, 128) for d in range(8)], axis=1)
-    down_ref[...] = dot(lhs, gather_ref[chip]).astype(BF16)
+    down_ref[0] = dot(lhs, gather_ref[chip]).reshape(4, 4, 4, WIDE).astype(BF16)
     arrived([c_copy, g_copy])
     for copies in (
-        meta_copies, v_copies, og_copies, w_copies, h_copies, g_copies, r_copies, x_copies,
+        meta_copies, v_copies, og_copies, dw_copies, cw_copies, h_copies, g_copies, r_copies, x_copies,
         d_copies, [c_copy, g_copy],
     ):
         for copy in copies:
@@ -614,12 +685,9 @@
 
 
 def fused(video, conv_weight, down_weight, out_grad, clip_bucket, start_frame, bucket_res):
-    bucket_ids = jnp.arange(bucket_res.shape[0], dtype=jnp.int32)
-    picked = (clip_bucket[:, None] == bucket_ids[None, :]).astype(jnp.int32)
-    limits = jnp.sum(picked[:, :, None] * bucket_res[None, :, :], axis=1)
-    facts = jnp.concatenate([start_frame, limits[0], jnp.zeros((5,), jnp.int32)]).astype(F32)
-    meta = jnp.broadcast_to(facts[:, None], (8, 128))
     vmem = pl.BlockSpec(memory_space=pltpu.VMEM)
+    smem = pl.BlockSpec(memory_space=pltpu.SMEM)
+    anywhere = pl.BlockSpec(memory_space=pl.ANY)
     full = pltpu.VMEM((10, 10, 32, WIDE), BF16)
     gathered = pltpu.VMEM((8, 512, 128), BF16)
     wide = pltpu.VMEM((512, 128), F32)
@@ -627,14 +695,20 @@
     down, video_grad, conv_grad, down_grad = pl.pallas_call(
         block_kernel,
         out_shape=(
-            jax.ShapeDtypeStruct((64, WIDE), BF16),
+            jax.ShapeDtypeStruct(out_grad.shape, BF16),
             jax.ShapeDtypeStruct((256, WIDE), BF16),
             jax.ShapeDtypeStruct(conv_weight.shape, F32),
             jax.ShapeDtypeStruct(down_weight.shape, F32),
         ),
-        in_specs=[vmem] * 8,
+        in_specs=[smem] * 3 + [vmem, anywhere, anywhere, vmem] + [anywhere] * 3,
         out_specs=(vmem,) * 4,
         scratch_shapes=[
+            pltpu.VMEM((8, 128), F32),
+            pltpu.VMEM(conv_weight.shape, BF16),
+            pltpu.VMEM(down_weight.shape, BF16),
+            pltpu.VMEM((512, 512), BF16),
+            pltpu.VMEM((4, 1024, 256), BF16),
+            pltpu.VMEM((768, 512), BF16),
             pltpu.VMEM((4, 8, 128), F32),
             piece,
             piece,
@@ -660,23 +734,26 @@
             pltpu.VMEM((8, 128, 256), BF16),
             pltpu.VMEM((8, 128, 128), BF16),
             wide,
-            pltpu.SemaphoreType.DMA((10, 8)),
-            pltpu.SemaphoreType.DMA((10, 8)),
+            pltpu.SemaphoreType.DMA((5,)),
+            pltpu.SemaphoreType.DMA((11, 8)),
+            pltpu.SemaphoreType.DMA((11, 8)),
         ],
         compiler_params=pltpu.CompilerParams(
-            collective_id=0, has_side_effects=True, vmem_limit_bytes=50 * 2**20
+            collective_id=0, has_side_effects=True, vmem_limit_bytes=60 * 2**20
         ),
     )(
-        meta,
+        clip_bucket,
+        start_frame,
+        bucket_res,
         video.reshape(256, WIDE),
         conv_weight,
         down_weight,
-        out_grad.reshape(64, WIDE),
+        out_grad,
         lane_swap(),
         lane_gather(),
         column_pick(),
     )
-    return (down.reshape(out_grad.shape), video_grad.reshape(video.shape), conv_grad, down_grad)
+    return (down, video_grad.reshape(video.shape), conv_grad, down_grad)
 
 
 def solution(mesh):

time: 79.5 us -> 59.4 us (0.75)
  Pallas kernels: 66.4 us -> 49.3 us
  local copies, waits for them, and re-layouts: 9.81 us -> 7.97 us
  other arithmetic: 0.88 us -> 0 us
    pallas_call x1, Pallas kernels: 66.4 us -> 49.3 us  [fused(): pl.pallas_call(block_kernel, out_shape=(jax.ShapeDtypeStruct(out_grad.sha...]
    reshape x2 -> x0, local copies, waits for them, and re-layouts: 1.4 us -> none  [the longest x1 0.78 us: fused(): out_grad.reshape(64, WIDE)]
    reduce_sum x1 -> x0, other arithmetic: 0.8 us -> none  [fused(): limits = jnp.sum(picked[:, :, None] * bucket_res[None, :, :], axis=1)]
    unnamed x11 -> x7, local copies, waits for them, and re-layouts: 8.33 us -> 7.97 us
where the time goes in v2:
time: 59.4 us; the launch traced here: 59.2 us
  Pallas kernels  49.3 us (83%)
  local copies, waits for them, and re-layouts  7.97 us (13%)
  between operations  1.93 us (3%)
    pallas_call x1, Pallas kernels, fused(): pl.pallas_call(block_kernel, out_shape=(jax.ShapeDtypeStruct(out_grad.sha...  49.3 us
    unnamed x7, local copies, waits for them, and re-layouts  7.97 us

profile of v2, /device:TPU:0, one launch (start us, length us, event | category | flops | bytes accessed | tf_op | source)
XLA Modules:
  0.0 59.2 jit_solution(16846146017797276892)
XLA Ops:
  1.9 1.3 %copy.14.res_table_ref = s32[4,2]{1,0:T(4,128)} copy(s32[4,2]{0,1:T(2,128)} %param.16) | data formatting | bytes 64 | tf_op args[6]
  3.3 49.3 %shard_map.129 = (bf16[1,4,4,4,256]{4,3,2,1,0:T(4,128)(2,1)}, bf16[256,256]{1,0:T(8,128)(2,1)}, f32[64,6912]{1,0:T(8,128)}, f32[64,2304]{1,0:T(8,128)}) custom-call(s32[1]{0:T(128)S(6)} %copy.19.bucket_ref, s32[1]{0:T(128)S(6)} %copy.20.start_ref, s32[4,2]{1,0:T(4,128)} %copy.14.res_table_ref, bf16[256,256]{1,0:T(8,128)(2,1)} %bitcast.2, ...), custom_call_target="tpu_custom_call" | custom-call | tf_op jit(solution)/shard_map/pallas_call | solution.py:695
  52.5 1.4 %copy.21 = bf16[1,4,4,4,256]{4,3,2,1,0:T(4,128)(2,1)} copy(bf16[1,4,4,4,256]{4,3,2,1,0:T(4,128)(2,1)} %get-tuple-element.16) | data formatting | bytes 65536
  53.9 1.6 %copy.22 = bf16[1,4,8,8,256]{4,3,2,1,0:T(8,128)(2,1)} copy(bf16[1,4,8,8,256]{4,3,2,1,0:T(8,128)(2,1)} %bitcast.3) | data formatting | bytes 262144
  55.5 0.0 copy-start
  55.5 2.9 %copy.23 = f32[64,6912]{1,0:T(8,128)} copy(f32[64,6912]{1,0:T(8,128)} %get-tuple-element.18) | data formatting | bytes 3538944
  58.3 0.0 copy-done
  58.3 0.8 %copy.24 = f32[64,2304]{1,0:T(8,128)} copy(f32[64,2304]{1,0:T(8,128)S(1)} %copy-done) | data formatting | bytes 1179648
Async XLA Ops:
  55.5 2.9 %copy-start = (f32[64,2304]{1,0:T(8,128)S(1)}, f32[64,2304]{1,0:T(8,128)}, u32[]{:S(2)}) copy-start(f32[64,2304]{1,0:T(8,128)} %get-tuple-element.19) | copy-start | bytes 1769476

commit v3 on v2

--- a/solution.py
+++ b/solution.py
@@ -239,14 +239,6 @@
     return jnp.asarray(table, BF16)
 
 
-def lane_gather():
-    lane = np.arange(1024)
-    owner, part, channel = lane // 128, lane // 32 % 4, lane % 32
-    table = np.zeros((4, 1024, 256), np.float32)
-    table[part, lane, owner * 32 + channel] = 1.0
-    return jnp.asarray(table, BF16)
-
-
 def column_pick():
     table = np.zeros((2, 3, 256, 4, 4, 32), np.float32)
     for core in range(2):
@@ -299,13 +291,23 @@
     return jnp.dot(wide, same, preferred_element_type=F32, precision=lax.Precision.HIGHEST)[0:1]
 
 
+def gathered_lanes(pieces, swap):
+    halves = [
+        dot(jnp.concatenate(pieces[4 * half : 4 * half + 4], axis=1), swap) for half in range(2)
+    ]
+    return [
+        jnp.concatenate([half[:, 128 * p : 128 * p + 128] for half in halves], axis=1)
+        for p in range(4)
+    ]
+
+
 def block_kernel(
     bucket_ref, start_ref, res_table_ref, video_ref, cw_hbm, dw_hbm, og_ref, swap_hbm,
-    gather_hbm, pick_hbm,
-    down_ref, vgrad_ref, cgrad_ref, dgrad_ref,
-    meta_ref, cw_ref, dw_ref, swap_ref, gather_ref, pick_ref,
-    meta_all, v_send, v_all, w_send, w_all, og_all, h_all, g_all, r_all, d_send, d_all,
-    x_send, x_all, h_full, g_full, r_full, og_up, rows_fwd, cells, normed_ref, mask_ref,
+    pick_hbm,
+    x_all, d_all, h_out, r_out, stack_out, og_stack_out,
+    meta_ref, cw_ref, dw_ref, swap_ref, pick_ref,
+    meta_all, v_send, v_all, w_send, w_all, og_all, h_all, g_all, r_all, d_send,
+    x_send, h_full, g_full, r_full, og_up, rows_fwd, cells, normed_ref, mask_ref,
     res_ref, stack_t, og_stack_t, back_ref, load_sems, send_sems, recv_sems,
 ):
     chip = lax.axis_index("fsdp")
@@ -323,7 +325,6 @@
             ("dw", dw_hbm, dw_ref),
             ("pick", pick_hbm.at[core], pick_ref),
             ("cw", cw_hbm, cw_ref),
-            ("gather", gather_hbm, gather_ref),
         )
     ):
         loads[name] = pltpu.make_async_copy(source, target, load_sems.at[index])
@@ -370,9 +371,9 @@
 
     bucket = bucket_ref[0]
     high, width = jnp.int32(0), jnp.int32(0)
-    for index in range(res_table_ref.shape[0]):
-        high = high + jnp.where(bucket == index, res_table_ref[index, 0], 0)
-        width = width + jnp.where(bucket == index, res_table_ref[index, 1], 0)
+    for index in range(res_table_ref.shape[1]):
+        high = high + jnp.where(bucket == index, res_table_ref[0, index], 0)
+        width = width + jnp.where(bucket == index, res_table_ref[1, index], 0)
     line = lax.broadcasted_iota(jnp.int32, (8, 128), 0)
     facts = jnp.where(line == 0, start_ref[0], jnp.where(line == 1, high, width)).astype(F32)
     meta_ref[...] = facts
@@ -515,54 +516,41 @@
             full[t + off, 9] = jnp.zeros((32, WIDE), BF16)
         r_full[t, 4, 0] = jnp.zeros((32, WIDE), BF16)
 
-    def stack_frame(t, carry):
-        at = pl.ds(pl.multiple_of(64 * t, 64), 64)
-        wide = res_ref[at, :]
-        shifts = [move_cols(wide, 1 - tap) for tap in range(3)]
-        place = lax.broadcasted_iota(jnp.int32, (64, 128), 1) // OWN
-        split = []
-        for clip in range(4):
-            block = jnp.zeros((64, 128), F32)
-            for tap in range(3):
-                turn = (OWN * (tap - clip)) % 128
-                moved = pltpu.roll(shifts[tap], turn, 1) if turn else shifts[tap]
-                block = jnp.where(place == tap, moved, block)
-            split.append(block.reshape(8, 8, 128))
-        rows = jnp.concatenate(split, axis=1).reshape(256, 128)
-        stack_t[t] = rows.T.astype(BF16)
+    def og_frame(t, carry):
+        from_row = lax.broadcasted_iota(jnp.int32, (WIDE, WIDE), 0)
+        to_lane = lax.broadcasted_iota(jnp.int32, (WIDE, WIDE), 1)
+        chosen = (from_row == to_lane % 64 + 64 * chip).astype(F32).astype(BF16)
+        rows = dot(og_up[t].reshape(128, WIDE), chosen)
+        tap = lax.broadcasted_iota(jnp.int32, (128, WIDE), 1) // 64
+        once, twice = move_cols(rows, -1), move_cols(rows, -2)
+        rows = jnp.where(tap == 0, rows, jnp.where(tap == 1, once, twice))
+        og_stack_t[t] = rows.T.astype(BF16)
         return carry
 
-    lax.fori_loop(0, 8, stack_frame, 0)
-
-    def og_frame(t, carry):
-        lhs = og_up[t].reshape(128, WIDE)
-        from_row = lax.broadcasted_iota(jnp.int32, (WIDE, 128), 0)
-        to_lane = lax.broadcasted_iota(jnp.int32, (WIDE, 128), 1)
-        total = None
-        for tap in range(3):
-            chosen = (to_lane // OWN == tap) & (from_row == to_lane % OWN + OWN * me)
-            term = move_cols(dot(lhs, chosen.astype(F32).astype(BF16)), -tap)
-            total = term if total is None else total + term
-        og_stack_t[t] = total.T.astype(BF16)
+    lax.fori_loop(0, 8, og_frame, 0)
+
+    def keep(index, source, target):
+        copy = pltpu.make_async_copy(source, target, load_sems.at[index])
+        copy.start()
+        return copy
+
+    kept = [keep(4, og_stack_t, og_stack_out)]
+
+    def assemble(source, t):
+        at = pl.ds(pl.multiple_of(256 * t, 256), 256)
+        clips = gathered_lanes([source[d, at, :] for d in range(8)], swap_ref[...])
+        blocks = [clip.reshape(32, 8, WIDE) for clip in clips]
+        return jnp.concatenate(blocks, axis=1).astype(BF16).reshape(4, 8, 32, WIDE)
+
+    relay(4, h_all, h_copies)
+    complete(h_copies)
+
+    def fill_hidden(t, carry):
+        h_full[pl.ds(4 * t + 2, 4), 1:9] = assemble(h_all, t)
         return carry
 
-    lax.fori_loop(0, 8, og_frame, 0)
-
-    def assemble(source, t):
-        at = pl.ds(pl.multiple_of(128 * t, 128), 128)
-        lhs = jnp.concatenate([source[d, at, :] for d in range(8)], axis=1)
-        blocks = [dot(lhs, gather_ref[clip]).reshape(16, 8, WIDE) for clip in range(4)]
-        return jnp.concatenate(blocks, axis=1).astype(BF16).reshape(2, 8, 32, WIDE)
-
-    relay(4, h_all, h_copies)
-    loads["gather"].wait()
-    complete(h_copies)
-
-    def fill_hidden(t, carry):
-        h_full[pl.ds(2 * t + 2, 2), 1:9] = assemble(h_all, t)
-        return carry
-
-    lax.fori_loop(0, 4, fill_hidden, 0)
+    lax.fori_loop(0, 2, fill_hidden, 0)
+    kept.append(keep(5, h_full, h_out))
 
     def conv_frame(t, carry):
         total = None
@@ -584,10 +572,10 @@
     complete(g_copies)
 
     def fill_grad(t, carry):
-        g_full[pl.ds(2 * t, 2), 1:9] = assemble(g_all, t)
+        g_full[pl.ds(4 * t, 4), 1:9] = assemble(g_all, t)
         return carry
 
-    lax.fori_loop(0, 4, fill_grad, 0)
+    lax.fori_loop(0, 2, fill_grad, 0)
 
     arrived(cw_copies)
 
@@ -621,23 +609,41 @@
     x_copies = send_all(8, lambda to: x_send.at[to], x_all.at[me])
 
     relay(6, r_all, r_copies)
-    lhs = jnp.concatenate([stack_t[t] for t in range(8)], axis=1)
-    for a in range(3):
-        for b in range(3):
-            rhs = h_full[a : a + 8, b : b + 8].reshape(2048, WIDE)
-            grad = dot(lhs, rhs)
+    place = lax.broadcasted_iota(jnp.int32, (64, 128), 1) // OWN
+
+    def stack_frame(t, carry):
+        at = pl.ds(pl.multiple_of(64 * t, 64), 64)
+        moved = []
+        for c in range(2):
+            block = g_all[2 * chip + c, at, :].astype(F32)
+            moved.append([move_cols(block, 1 - tap) for tap in range(3)])
+        split = []
+        for clip in range(4):
+            sides = [jnp.zeros((64, 128), F32)] * 2
             for tap in range(3):
-                at = (9 * a + 3 * b + tap) * WIDE
-                cgrad_ref[mine, at : at + WIDE] = grad[32 * tap : 32 * tap + 32]
-    c_copy = send(9, 0, cgrad_ref.at[mine], cgrad_ref.at[mine], sibling)
+                for c in range(2):
+                    spot = 2 * (tap % 2) + c
+                    turn = (OWN * (spot - clip)) % 128
+                    block = moved[c][tap]
+                    if turn:
+                        block = pltpu.roll(block, turn, 1)
+                    sides[tap // 2] = jnp.where(place == spot, block, sides[tap // 2])
+            split.append(jnp.concatenate(sides, axis=1).reshape(8, 8, WIDE))
+        rows = jnp.concatenate(split, axis=1).reshape(256, WIDE)
+        stack_t[t] = rows.T.astype(BF16)
+        return carry
+
+    lax.fori_loop(0, 8, stack_frame, 0)
+    kept.append(keep(6, stack_t, stack_out))
 
     complete(r_copies)
 
     def fill_residual(t, carry):
-        r_full[pl.ds(2 * t, 2), 0:4] = assemble(r_all, t).reshape(2, 4, 2, 32, WIDE)
+        r_full[pl.ds(4 * t, 4), 0:4] = assemble(r_all, t).reshape(4, 4, 2, 32, WIDE)
         return carry
 
-    lax.fori_loop(0, 4, fill_residual, 0)
+    lax.fori_loop(0, 2, fill_residual, 0)
+    kept.append(keep(7, r_full, r_out))
 
     def down_frame(t, carry):
         total = None
@@ -659,29 +665,75 @@
 
     d_all[me] = d_send[frames_of(me)]
     d_copies = send_all(7, lambda to: d_send.at[frames_of(to)], d_all.at[me])
-    lhs = jnp.concatenate([og_stack_t[t] for t in range(8)], axis=1)
-    for b in range(3):
-        rhs = r_full[:, b // 2 : b // 2 + 4, b % 2].reshape(1024, WIDE)
-        grad = dot(lhs, rhs)
-        for tap in range(3):
-            at = (3 * b + tap) * WIDE
-            dgrad_ref[mine, at : at + WIDE] = grad[32 * tap : 32 * tap + 32]
-    g_copy = send(9, 1, dgrad_ref.at[mine], dgrad_ref.at[mine], sibling)
-
     arrived(x_copies)
-    lhs = jnp.concatenate([x_all[d] for d in range(8)], axis=1)
-    for t in range(4):
-        vgrad_ref[64 * t : 64 * t + 64, :] = dot(lhs, gather_ref[t]).astype(BF16)
     arrived(d_copies)
-    lhs = jnp.concatenate([d_all[d].reshape(64, 128) for d in range(8)], axis=1)
-    down_ref[0] = dot(lhs, gather_ref[chip]).reshape(4, 4, 4, WIDE).astype(BF16)
-    arrived([c_copy, g_copy])
+    for copy in kept:
+        copy.wait()
     for copies in (
         meta_copies, v_copies, og_copies, dw_copies, cw_copies, h_copies, g_copies, r_copies, x_copies,
-        d_copies, [c_copy, g_copy],
+        d_copies,
     ):
         for copy in copies:
             copy.wait_send()
+
+
+def finish_kernel(
+    x_hbm, d_hbm, h_hbm, r_hbm, stack_hbm, og_stack_hbm, swap_hbm,
+    down_ref, vgrad_ref, cgrad_hbm, dgrad_hbm,
+    x_all, d_all, h_full, r_full, stack_t, og_stack_t, swap_ref, cgrad_ref, dgrad_ref,
+    load_sems, store_sems,
+):
+    chip = lax.axis_index("fsdp")
+    loads = []
+    for index, (source, target) in enumerate(
+        (
+            (swap_hbm, swap_ref),
+            (x_hbm, x_all),
+            (d_hbm, d_all),
+            (stack_hbm, stack_t),
+            (h_hbm, h_full),
+            (og_stack_hbm, og_stack_t),
+            (r_hbm, r_full),
+        )
+    ):
+        loads.append(pltpu.make_async_copy(source, target, load_sems.at[index]))
+        loads[-1].start()
+    for copy in loads[:3]:
+        copy.wait()
+    frames = gathered_lanes([x_all[d] for d in range(8)], swap_ref[...])
+    for t, block in enumerate(frames):
+        vgrad_ref[64 * t : 64 * t + 64, :] = block.astype(BF16)
+    clips = gathered_lanes([d_all[d].reshape(64, 128) for d in range(8)], swap_ref[...])
+    own = clips[0]
+    for clip in range(1, 4):
+        own = jnp.where(chip == clip, clips[clip], own)
+    down_ref[0] = own.reshape(4, 4, 4, WIDE).astype(BF16)
+
+    stores = []
+
+    def put(grad, ref, hbm, block, index):
+        for tap in range(3):
+            at = (3 * block + tap) * WIDE
+            ref[:, at : at + WIDE] = grad[64 * tap : 64 * tap + 64]
+        part = pl.ds(3 * block * WIDE, 3 * WIDE)
+        stores.append(pltpu.make_async_copy(ref.at[:, part], hbm.at[:, part], store_sems.at[index]))
+        stores[-1].start()
+
+    loads[3].wait()
+    loads[4].wait()
+    lhs = jnp.concatenate([stack_t[t, 0:192] for t in range(8)], axis=1)
+    for a in range(3):
+        for b in range(3):
+            rhs = h_full[a : a + 8, b : b + 8].reshape(2048, WIDE)
+            put(dot(lhs, rhs), cgrad_ref, cgrad_hbm, 3 * a + b, 3 * a + b)
+    loads[5].wait()
+    loads[6].wait()
+    lhs = jnp.concatenate([og_stack_t[t, 0:192] for t in range(8)], axis=1)
+    for b in range(3):
+        rhs = r_full[:, b // 2 : b // 2 + 4, b % 2].reshape(1024, WIDE)
+        put(dot(lhs, rhs), dgrad_ref, dgrad_hbm, b, 9 + b)
+    for copy in stores:
+        copy.wait()
 
 
 def fused(video, conv_weight, down_weight, out_grad, clip_bucket, start_frame, bucket_res):
@@ -692,22 +744,23 @@
     gathered = pltpu.VMEM((8, 512, 128), BF16)
     wide = pltpu.VMEM((512, 128), F32)
     piece = pltpu.VMEM((8, 64, 128), BF16)
-    down, video_grad, conv_grad, down_grad = pl.pallas_call(
+    sent = jax.ShapeDtypeStruct((8, 64, 128), BF16)
+    sent_down = jax.ShapeDtypeStruct((8, 4, 16, 128), BF16)
+    full_cells = jax.ShapeDtypeStruct((10, 10, 32, WIDE), BF16)
+    even_cells = jax.ShapeDtypeStruct((8, 5, 2, 32, WIDE), BF16)
+    stack = jax.ShapeDtypeStruct((8, 256, 256), BF16)
+    og_stack = jax.ShapeDtypeStruct((8, 256, 128), BF16)
+    swap = lane_swap()
+    parts = pl.pallas_call(
         block_kernel,
-        out_shape=(
-            jax.ShapeDtypeStruct(out_grad.shape, BF16),
-            jax.ShapeDtypeStruct((256, WIDE), BF16),
-            jax.ShapeDtypeStruct(conv_weight.shape, F32),
-            jax.ShapeDtypeStruct(down_weight.shape, F32),
-        ),
-        in_specs=[smem] * 3 + [vmem, anywhere, anywhere, vmem] + [anywhere] * 3,
-        out_specs=(vmem,) * 4,
+        out_shape=(sent, sent_down, full_cells, even_cells, stack, og_stack),
+        in_specs=[smem] * 3 + [vmem, anywhere, anywhere, vmem] + [anywhere] * 2,
+        out_specs=(vmem,) * 2 + (anywhere,) * 4,
         scratch_shapes=[
             pltpu.VMEM((8, 128), F32),
             pltpu.VMEM(conv_weight.shape, BF16),
             pltpu.VMEM(down_weight.shape, BF16),
             pltpu.VMEM((512, 512), BF16),
-            pltpu.VMEM((4, 1024, 256), BF16),
             pltpu.VMEM((768, 512), BF16),
             pltpu.VMEM((4, 8, 128), F32),
             piece,
@@ -719,8 +772,6 @@
             gathered,
             gathered,
             pltpu.VMEM((8, 16, 128), BF16),
-            pltpu.VMEM((8, 4, 16, 128), BF16),
-            piece,
             piece,
             full,
             full,
@@ -731,10 +782,10 @@
             wide,
             wide,
             wide,
-            pltpu.VMEM((8, 128, 256), BF16),
-            pltpu.VMEM((8, 128, 128), BF16),
+            pltpu.VMEM((8, 256, 256), BF16),
+            pltpu.VMEM((8, 256, 128), BF16),
             wide,
-            pltpu.SemaphoreType.DMA((5,)),
+            pltpu.SemaphoreType.DMA((8,)),
             pltpu.SemaphoreType.DMA((11, 8)),
             pltpu.SemaphoreType.DMA((11, 8)),
         ],
@@ -744,15 +795,34 @@
     )(
         clip_bucket,
         start_frame,
-        bucket_res,
+        bucket_res.T,
         video.reshape(256, WIDE),
         conv_weight,
         down_weight,
         out_grad,
-        lane_swap(),
-        lane_gather(),
+        swap,
         column_pick(),
     )
+    kinds = (sent, sent_down, full_cells, even_cells, stack, og_stack, swap)
+    down, video_grad, conv_grad, down_grad = pl.pallas_call(
+        finish_kernel,
+        out_shape=(
+            jax.ShapeDtypeStruct(out_grad.shape, BF16),
+            jax.ShapeDtypeStruct((256, WIDE), BF16),
+            jax.ShapeDtypeStruct(conv_weight.shape, F32),
+            jax.ShapeDtypeStruct(down_weight.shape, F32),
+        ),
+        in_specs=[anywhere] * 7,
+        out_specs=(vmem, vmem, anywhere, anywhere),
+        scratch_shapes=[pltpu.VMEM(kind.shape, BF16) for kind in kinds]
+        + [
+            pltpu.VMEM(conv_weight.shape, F32),
+            pltpu.VMEM(down_weight.shape, F32),
+            pltpu.SemaphoreType.DMA((7,)),
+            pltpu.SemaphoreType.DMA((12,)),
+        ],
+        compiler_params=pltpu.CompilerParams(vmem_limit_bytes=60 * 2**20),
+    )(*parts, swap)
     return (down, video_grad.reshape(video.shape), conv_grad, down_grad)
 
 

time: 59.4 us -> 56.1 us (0.944)
  local copies, waits for them, and re-layouts: 7.97 us -> 0 us
  Pallas kernels: 49.3 us -> 54 us
    unnamed x7 -> x0, local copies, waits for them, and re-layouts: 7.97 us -> none
    pallas_call x1 -> x2, Pallas kernels: 49.3 us -> 54 us  [the longest x1 47.7 us: fused(): pl.pallas_call(block_kernel, out_shape=(sent, sent_down, full_cells, even...]
where the time goes in v3:
time: 56.1 us; the launch traced here: 55.9 us
  Pallas kernels  54 us (96%)
  between operations  1.93 us (3%)
    pallas_call x1, Pallas kernels, fused(): pl.pallas_call(block_kernel, out_shape=(sent, sent_down, full_cells, even...  47.7 us
    pallas_call x1, Pallas kernels, fused(): pl.pallas_call(finish_kernel, out_shape=(jax.ShapeDtypeStruct(out_grad.sh...  6.27 us

profile of v3, /device:TPU:0, one launch (start us, length us, event | category | flops | bytes accessed | tf_op | source)
XLA Modules:
  0.0 55.9 jit_solution(16234697087624959017)
XLA Ops:
  1.9 47.7 %shard_map.120 = (bf16[8,64,128]{2,1,0:T(8,128)(2,1)}, bf16[8,4,16,128]{3,2,1,0:T(8,128)(2,1)}, bf16[10,10,32,256]{3,2,1,0:T(8,128)(2,1)}, bf16[8,5,2,32,256]{4,...) custom-call(s32[1]{0:T(128)S(6)} %copy.13.bucket_ref, s32[1]{0:T(128)S(6)} %copy.14.start_ref, ...), custom_call_target="tpu_custom_call" | custom-call | tf_op jit(solution)/shard_map/pallas_call | solution.py:754
  49.6 6.3 %shard_map.121 = (bf16[1,4,4,4,256]{4,3,2,1,0:T(4,128)(2,1)}, bf16[256,256]{1,0:T(8,128)(2,1)}, f32[64,6912]{1,0:T(8,128)}, f32[64,2304]{1,0:T(8,128)}) custom-call(bf16[8,64,128]{2,1,0:T(8,128)(2,1)} %get-tuple-element.14.x_hbm, bf16[8,4,16,128]{3,2,1,0:T(8,128)(2,1)} %get-tuple-element.15.d_hbm, bf16[10,10,32,256]{3,2,1,0:T(8,128)(2,1)} %get-tuple-element.16.h_hbm, ...), custom_call_target="tpu_custom_call" | custom-call | tf_op jit(solution)/shard_map/pallas_call | solution.py:807

commit v4 on v3

--- a/solution.py
+++ b/solution.py
@@ -307,7 +307,7 @@
     x_all, d_all, h_out, r_out, stack_out, og_stack_out,
     meta_ref, cw_ref, dw_ref, swap_ref, pick_ref,
     meta_all, v_send, v_all, w_send, w_all, og_all, h_all, g_all, r_all, d_send,
-    x_send, h_full, g_full, r_full, og_up, rows_fwd, cells, normed_ref, mask_ref,
+    x_send, p_send, p_all, h_full, g_full, r_full, rows_back, og_up, rows_fwd, cells, normed_ref, mask_ref,
     res_ref, stack_t, og_stack_t, back_ref, load_sems, send_sems, recv_sems,
 ):
     chip = lax.axis_index("fsdp")
@@ -402,26 +402,19 @@
     loads["dw"].wait()
     loads["pick"].wait()
 
-    def exchange_columns(phase, ref, blocks, first):
-        picks = None
-        for tap in range(3):
-            at = [(3 * block + tap) * WIDE for block in range(blocks)]
-            rows = jnp.concatenate([ref[:, low : low + WIDE] for low in at], axis=0)
-            term = dot(rows, pick_ref[256 * tap : 256 * tap + 256, :])
-            picks = term if picks is None else picks + term
-        part = pl.ds(first, 64 * blocks)
-        for other in range(4):
-            w_send[other, part, :] = picks[:, 128 * other : 128 * other + 128].astype(BF16)
-        w_all[chip, part, :] = w_send[chip, part, :]
-        copies = []
-        for s in range(1, 4):
-            to = (chip + s) % 4
-            copies.append(
-                send(phase, s, w_send.at[to, part], w_all.at[chip, part], to * 2 + core)
-            )
-        return copies
-
-    dw_copies = exchange_columns(2, dw_ref, 3, 576)
+    picks = None
+    for tap in range(3):
+        at = [(3 * b + tap) * WIDE for b in range(3)]
+        rows = jnp.concatenate([dw_ref[:, low : low + WIDE] for low in at], axis=0)
+        term = dot(rows, pick_ref[256 * tap : 256 * tap + 256, :])
+        picks = term if picks is None else picks + term
+    for other in range(4):
+        w_send[other] = picks[:, 128 * other : 128 * other + 128].astype(BF16)
+    w_all[chip] = w_send[chip]
+    dw_copies = []
+    for s in range(1, 4):
+        to = (chip + s) % 4
+        dw_copies.append(send(2, s, w_send.at[to], w_all.at[chip], to * 2 + core))
 
     arrived(meta_copies)
     place1 = lax.broadcasted_iota(jnp.int32, (1, 128), 1) // OWN
@@ -477,7 +470,7 @@
         lhs = og_up[t].reshape(128, WIDE)
         layers = []
         for b in range(3):
-            panel = w_all[:, 64 * (9 + b) : 64 * (10 + b), :].reshape(256, 128)
+            panel = w_all[:, 64 * b : 64 * b + 64, :].reshape(256, 128)
             layers.append(fold_taps(dot(lhs, panel), 4, (0, -1, -2)).reshape(4, 8, 128))
         even = layers[0] + jnp.concatenate([jnp.zeros((1, 8, 128), F32), layers[2][:3]], axis=0)
         both = jnp.stack([even, layers[1]], axis=1).reshape(64, 128)
@@ -489,10 +482,18 @@
         return carry
 
     lax.fori_loop(0, 8, res_grad_frame, 0)
-    g_copies = spread_out(5, g_all)
+    g_copies = [send(5, 0, g_all.at[me], g_all.at[me], sibling)]
 
     loads["cw"].wait()
-    cw_copies = exchange_columns(10, cw_ref, 9, 0)
+    from_row = lax.broadcasted_iota(jnp.int32, (WIDE, 128), 0)
+    to_lane = lax.broadcasted_iota(jnp.int32, (WIDE, 128), 1)
+    chosen = from_row == to_lane // OWN * 64 + OWN * core + to_lane % OWN
+    chosen = chosen.astype(F32).astype(BF16)
+    for ab in range(9):
+        at = [(3 * ab + tap) * WIDE for tap in range(3)]
+        rows = jnp.concatenate([cw_ref[:, low : low + WIDE] for low in at], axis=0)
+        rows_back[ab, 0:192, :] = dot(rows, chosen).astype(BF16)
+        rows_back[ab, 192:256, :] = jnp.zeros((64, 128), BF16)
 
     mine = pl.ds(pl.multiple_of(core * OWN, OWN), OWN)
     for ab in range(9):
@@ -516,99 +517,7 @@
             full[t + off, 9] = jnp.zeros((32, WIDE), BF16)
         r_full[t, 4, 0] = jnp.zeros((32, WIDE), BF16)
 
-    def og_frame(t, carry):
-        from_row = lax.broadcasted_iota(jnp.int32, (WIDE, WIDE), 0)
-        to_lane = lax.broadcasted_iota(jnp.int32, (WIDE, WIDE), 1)
-        chosen = (from_row == to_lane % 64 + 64 * chip).astype(F32).astype(BF16)
-        rows = dot(og_up[t].reshape(128, WIDE), chosen)
-        tap = lax.broadcasted_iota(jnp.int32, (128, WIDE), 1) // 64
-        once, twice = move_cols(rows, -1), move_cols(rows, -2)
-        rows = jnp.where(tap == 0, rows, jnp.where(tap == 1, once, twice))
-        og_stack_t[t] = rows.T.astype(BF16)
-        return carry
-
-    lax.fori_loop(0, 8, og_frame, 0)
-
-    def keep(index, source, target):
-        copy = pltpu.make_async_copy(source, target, load_sems.at[index])
-        copy.start()
-        return copy
-
-    kept = [keep(4, og_stack_t, og_stack_out)]
-
-    def assemble(source, t):
-        at = pl.ds(pl.multiple_of(256 * t, 256), 256)
-        clips = gathered_lanes([source[d, at, :] for d in range(8)], swap_ref[...])
-        blocks = [clip.reshape(32, 8, WIDE) for clip in clips]
-        return jnp.concatenate(blocks, axis=1).astype(BF16).reshape(4, 8, 32, WIDE)
-
-    relay(4, h_all, h_copies)
-    complete(h_copies)
-
-    def fill_hidden(t, carry):
-        h_full[pl.ds(4 * t + 2, 4), 1:9] = assemble(h_all, t)
-        return carry
-
-    lax.fori_loop(0, 2, fill_hidden, 0)
-    kept.append(keep(5, h_full, h_out))
-
-    def conv_frame(t, carry):
-        total = None
-        for a in range(3):
-            for b in range(3):
-                window = h_full[t + a, b : b + 8].reshape(256, WIDE)
-                term = dot_nt(window, rows_fwd[3 * a + b])
-                total = term if total is None else total + term
-        folded = fold_taps(total, 8, (-1, 0, 1))
-        at = pl.ds(pl.multiple_of(64 * t, 64), 64)
-        r_all[me, at, :] = (mask_ref[at, :] * (cells[at, :] + folded)).astype(BF16)
-        return carry
-
-    lax.fori_loop(0, 4, conv_frame, 0)
-    relay(5, g_all, g_copies)
-    lax.fori_loop(4, 8, conv_frame, 0)
-    r_copies = spread_out(6, r_all)
-
-    complete(g_copies)
-
-    def fill_grad(t, carry):
-        g_full[pl.ds(4 * t, 4), 1:9] = assemble(g_all, t)
-        return carry
-
-    lax.fori_loop(0, 2, fill_grad, 0)
-
-    arrived(cw_copies)
-
-    def back_frame(t, carry):
-        total = None
-        for a in range(3):
-            for b in range(3):
-                window = g_full[t + 2 - a, 2 - b : 10 - b].reshape(256, WIDE)
-                at = 64 * (3 * a + b)
-                term = dot(window, w_all[:, at : at + 64, :].reshape(256, 128))
-                total = term if total is None else total + term
-        at = pl.ds(pl.multiple_of(64 * t, 64), 64)
-        back_ref[at, :] = fold_taps(total, 8, (1, 0, -1))
-        return carry
-
-    lax.fori_loop(0, 8, back_frame, 0)
-    mask = mask_ref[...]
-    normed = normed_ref[...]
-    gate = 1.0 / (1.0 + jnp.exp(-normed))
-    pushed = mask * back_ref[...] * gate * (1.0 + normed * (1.0 - gate))
-    mean_push = group_total(jnp.sum(pushed, axis=0, keepdims=True)) / count
-    mean_pair = group_total(jnp.sum(pushed * normed, axis=0, keepdims=True)) / count
-    through = inverse * (pushed - mean_push - normed * mean_pair)
-    back_ref[...] = mask * through + res_ref[...]
-    for c in range(2):
-        quarter = [back_ref[64 * (4 * c + q) : 64 * (4 * c + q) + 64, :] for q in range(4)]
-        swapped = dot(jnp.concatenate(quarter, axis=1).astype(BF16), swap_ref[...]).astype(BF16)
-        for other in range(4):
-            x_send[2 * other + c] = swapped[:, 128 * other : 128 * other + 128]
-    x_all[me] = x_send[me]
-    x_copies = send_all(8, lambda to: x_send.at[to], x_all.at[me])
-
-    relay(6, r_all, r_copies)
+    arrived(g_copies)
     place = lax.broadcasted_iota(jnp.int32, (64, 128), 1) // OWN
 
     def stack_frame(t, carry):
@@ -630,10 +539,120 @@
                     sides[tap // 2] = jnp.where(place == spot, block, sides[tap // 2])
             split.append(jnp.concatenate(sides, axis=1).reshape(8, 8, WIDE))
         rows = jnp.concatenate(split, axis=1).reshape(256, WIDE)
+        g_full[t, 1:9] = rows.astype(BF16).reshape(8, 32, WIDE)
+        return carry
+
+    lax.fori_loop(0, 8, stack_frame, 0)
+
+    def back_frame(t, carry):
+        total = None
+        for a in range(3):
+            for b in range(3):
+                window = g_full[t + 2 - a, 2 - b : 10 - b].reshape(256, WIDE)
+                term = dot(window, rows_back[3 * a + b])
+                total = term if total is None else total + term
+        parts = total.reshape(8, 4, 8, 128)
+        at = pl.ds(pl.multiple_of(64 * t, 64), 64)
+        own = jnp.zeros((64, 128), F32)
+        for other in range(4):
+            piece = jnp.zeros((64, 128), F32)
+            for clip in range(4):
+                block = parts[:, clip].reshape(64, 128)
+                turn = (OWN * (clip - other)) % 128
+                if turn:
+                    block = pltpu.roll(block, turn, 1)
+                piece = jnp.where(place == clip, block, piece)
+            p_send[other, at, :] = piece.astype(BF16)
+            own = jnp.where(chip == other, piece, own)
+        back_ref[at, :] = own
+        return carry
+
+    lax.fori_loop(0, 5, back_frame, 0)
+    relay(4, h_all, h_copies)
+    lax.fori_loop(5, 8, back_frame, 0)
+    p_copies = []
+    for s in range(1, 4):
+        to = (chip + s) % 4
+        p_copies.append(send(10, s, p_send.at[to], p_all.at[s], to * 2 + core))
+
+    def assemble(source, t):
+        at = pl.ds(pl.multiple_of(256 * t, 256), 256)
+        clips = gathered_lanes([source[d, at, :] for d in range(8)], swap_ref[...])
+        blocks = [clip.reshape(32, 8, WIDE) for clip in clips]
+        return jnp.concatenate(blocks, axis=1).astype(BF16).reshape(4, 8, 32, WIDE)
+
+    def keep(index, source, target):
+        copy = pltpu.make_async_copy(source, target, load_sems.at[index])
+        copy.start()
+        return copy
+
+    kept = []
+
+    complete(h_copies)
+
+    def fill_hidden(t, carry):
+        h_full[pl.ds(4 * t + 2, 4), 1:9] = assemble(h_all, t)
+        return carry
+
+    lax.fori_loop(0, 2, fill_hidden, 0)
+    kept.append(keep(5, h_full, h_out))
+
+    def conv_frame(t, carry):
+        total = None
+        for a in range(3):
+            for b in range(3):
+                window = h_full[t + a, b : b + 8].reshape(256, WIDE)
+                term = dot_nt(window, rows_fwd[3 * a + b])
+                total = term if total is None else total + term
+        folded = fold_taps(total, 8, (-1, 0, 1))
+        at = pl.ds(pl.multiple_of(64 * t, 64), 64)
+        r_all[me, at, :] = (mask_ref[at, :] * (cells[at, :] + folded)).astype(BF16)
+        return carry
+
+    lax.fori_loop(0, 8, conv_frame, 0)
+    r_copies = spread_out(6, r_all)
+
+    arrived(p_copies)
+    mask = mask_ref[...]
+    normed = normed_ref[...]
+    gate = 1.0 / (1.0 + jnp.exp(-normed))
+    back = back_ref[...]
+    for s in range(1, 4):
+        back = back + p_all[s].astype(F32)
+    pushed = mask * back * gate * (1.0 + normed * (1.0 - gate))
+    mean_push = group_total(jnp.sum(pushed, axis=0, keepdims=True)) / count
+    mean_pair = group_total(jnp.sum(pushed * normed, axis=0, keepdims=True)) / count
+    through = inverse * (pushed - mean_push - normed * mean_pair)
+    back_ref[...] = mask * through + res_ref[...]
+    for c in range(2):
+        quarter = [back_ref[64 * (4 * c + q) : 64 * (4 * c + q) + 64, :] for q in range(4)]
+        swapped = dot(jnp.concatenate(quarter, axis=1).astype(BF16), swap_ref[...]).astype(BF16)
+        for other in range(4):
+            x_send[2 * other + c] = swapped[:, 128 * other : 128 * other + 128]
+    x_all[me] = x_send[me]
+    x_copies = send_all(8, lambda to: x_send.at[to], x_all.at[me])
+
+    def og_frame(t, carry):
+        from_row = lax.broadcasted_iota(jnp.int32, (WIDE, WIDE), 0)
+        to_lane = lax.broadcasted_iota(jnp.int32, (WIDE, WIDE), 1)
+        chosen = (from_row == to_lane % 64 + 64 * chip).astype(F32).astype(BF16)
+        rows = dot(og_up[t].reshape(128, WIDE), chosen)
+        tap = lax.broadcasted_iota(jnp.int32, (128, WIDE), 1) // 64
+        once, twice = move_cols(rows, -1), move_cols(rows, -2)
+        rows = jnp.where(tap == 0, rows, jnp.where(tap == 1, once, twice))
+        og_stack_t[t] = rows.T.astype(BF16)
+        return carry
+
+    lax.fori_loop(0, 8, og_frame, 0)
+
+    kept.append(keep(4, og_stack_t, og_stack_out))
+    relay(6, r_all, r_copies)
+    def turn_frame(t, carry):
+        rows = g_full[t, 1:9].reshape(256, WIDE).astype(F32)
         stack_t[t] = rows.T.astype(BF16)
         return carry
 
-    lax.fori_loop(0, 8, stack_frame, 0)
+    lax.fori_loop(0, 8, turn_frame, 0)
     kept.append(keep(6, stack_t, stack_out))
 
     complete(r_copies)
@@ -670,7 +689,7 @@
     for copy in kept:
         copy.wait()
     for copies in (
-        meta_copies, v_copies, og_copies, dw_copies, cw_copies, h_copies, g_copies, r_copies, x_copies,
+        meta_copies, v_copies, og_copies, dw_copies, p_copies, h_copies, g_copies, r_copies, x_copies,
         d_copies,
     ):
         for copy in copies:
@@ -765,17 +784,20 @@
             pltpu.VMEM((4, 8, 128), F32),
             piece,
             piece,
-            pltpu.VMEM((4, 768, 128), BF16),
-            pltpu.VMEM((4, 768, 128), BF16),
+            pltpu.VMEM((4, 192, 128), BF16),
+            pltpu.VMEM((4, 192, 128), BF16),
             pltpu.VMEM((8, 64, WIDE), BF16),
             gathered,
             gathered,
             gathered,
             pltpu.VMEM((8, 16, 128), BF16),
             piece,
+            pltpu.VMEM((4, 512, 128), BF16),
+            pltpu.VMEM((4, 512, 128), BF16),
             full,
             full,
             pltpu.VMEM((8, 5, 2, 32, WIDE), BF16),
+            pltpu.VMEM((9, 256, 128), BF16),
             pltpu.VMEM((8, 4, 32, WIDE), BF16),
             pltpu.VMEM((12, 128, WIDE), BF16),
             wide,

time: 56.1 us -> 55.6 us (level)
  no operation moved by 1% of the time
where the time goes in v4:
time: 55.6 us; the launch traced here: 55.5 us
  Pallas kernels  53.5 us (96%)
  between operations  1.93 us (3%)
    pallas_call x1, Pallas kernels, fused(): pl.pallas_call(block_kernel, out_shape=(sent, sent_down, full_cells, even...  47.3 us
    pallas_call x1, Pallas kernels, fused(): pl.pallas_call(finish_kernel, out_shape=(jax.ShapeDtypeStruct(out_grad.sh...  6.27 us

profile of v4, /device:TPU:0, one launch (start us, length us, event | category | flops | bytes accessed | tf_op | source)
XLA Modules:
  0.0 55.5 jit_solution(18311319051859051642)
XLA Ops:
  1.9 47.3 %shard_map.120 = (bf16[8,64,128]{2,1,0:T(8,128)(2,1)}, bf16[8,4,16,128]{3,2,1,0:T(8,128)(2,1)}, bf16[10,10,32,256]{3,2,1,0:T(8,128)(2,1)}, bf16[8,5,2,32,256]{4,...) custom-call(s32[1]{0:T(128)S(6)} %copy.13.bucket_ref, s32[1]{0:T(128)S(6)} %copy.14.start_ref, ...), custom_call_target="tpu_custom_call" | custom-call | tf_op jit(solution)/shard_map/pallas_call | solution.py:773
  49.2 6.3 %shard_map.121 = (bf16[1,4,4,4,256]{4,3,2,1,0:T(4,128)(2,1)}, bf16[256,256]{1,0:T(8,128)(2,1)}, f32[64,6912]{1,0:T(8,128)}, f32[64,2304]{1,0:T(8,128)}) custom-call(bf16[8,64,128]{2,1,0:T(8,128)(2,1)} %get-tuple-element.14.x_hbm, bf16[8,4,16,128]{3,2,1,0:T(8,128)(2,1)} %get-tuple-element.15.d_hbm, bf16[10,10,32,256]{3,2,1,0:T(8,128)(2,1)} %get-tuple-element.16.h_hbm, ...), custom_call_target="tpu_custom_call" | custom-call | tf_op jit(solution)/shard_map/pallas_call | solution.py:829

commit v5 on v4

--- a/solution.py
+++ b/solution.py
@@ -253,10 +253,6 @@
     return jnp.dot(lhs, rhs, preferred_element_type=F32)
 
 
-def dot_nt(lhs, rhs):
-    return lax.dot_general(lhs, rhs, (((1,), (1,)), ((), ())), preferred_element_type=F32)
-
-
 def move_cols(block, distance):
     if distance == 0:
         return block
@@ -307,7 +303,7 @@
     x_all, d_all, h_out, r_out, stack_out, og_stack_out,
     meta_ref, cw_ref, dw_ref, swap_ref, pick_ref,
     meta_all, v_send, v_all, w_send, w_all, og_all, h_all, g_all, r_all, d_send,
-    x_send, p_send, p_all, h_full, g_full, r_full, rows_back, og_up, rows_fwd, cells, normed_ref, mask_ref,
+    x_send, p_send, p_all, h_full, g_full, r_full, rows_back, rows_down, sums, og_up, rows_fwd, cells, normed_ref, mask_ref,
     res_ref, stack_t, og_stack_t, back_ref, load_sems, send_sems, recv_sems,
 ):
     chip = lax.axis_index("fsdp")
@@ -492,20 +488,22 @@
     for ab in range(9):
         at = [(3 * ab + tap) * WIDE for tap in range(3)]
         rows = jnp.concatenate([cw_ref[:, low : low + WIDE] for low in at], axis=0)
-        rows_back[ab, 0:192, :] = dot(rows, chosen).astype(BF16)
-        rows_back[ab, 192:256, :] = jnp.zeros((64, 128), BF16)
+        low = 128 * (ab // 3)
+        rows_back[ab % 3, 0:192, low : low + 128] = dot(rows, chosen).astype(BF16)
+        rows_back[ab % 3, 192:256, low : low + 128] = jnp.zeros((64, 128), BF16)
 
     mine = pl.ds(pl.multiple_of(core * OWN, OWN), OWN)
+    blank = jnp.zeros((32, WIDE), BF16)
+
+    def turned(ref, block):
+        rows = [ref[mine, (3 * block + c) * WIDE : (3 * block + c + 1) * WIDE] for c in range(3)]
+        return jnp.concatenate(rows + [blank], axis=0).T
+
     for ab in range(9):
-        for tap in range(3):
-            at = (3 * ab + tap) * WIDE
-            rows_fwd[ab, 32 * tap : 32 * tap + 32, :] = cw_ref[mine, at : at + WIDE]
-        rows_fwd[ab, 96:128, :] = jnp.zeros((32, WIDE), BF16)
+        low = 128 * (ab // 3)
+        rows_fwd[ab % 3, :, low : low + 128] = turned(cw_ref, ab)
     for b in range(3):
-        for tap in range(3):
-            at = (3 * b + tap) * WIDE
-            rows_fwd[9 + b, 32 * tap : 32 * tap + 32, :] = dw_ref[mine, at : at + WIDE]
-        rows_fwd[9 + b, 96:128, :] = jnp.zeros((32, WIDE), BF16)
+        rows_down[b] = turned(dw_ref, b)
 
     edge = jnp.zeros((10, 32, WIDE), BF16)
     for t in range(2):
@@ -544,13 +542,26 @@
 
     lax.fori_loop(0, 8, stack_frame, 0)
 
+    def three_taps(u, full, weights, shift, row_of):
+        total = None
+        for b in range(3):
+            low = row_of(b)
+            window = full[pl.ds(2 * u + shift, 2), low : low + 8].reshape(512, WIDE)
+            term = dot(window, weights[b])
+            total = term if total is None else total + term
+        return [
+            total[:, 128 * a : 128 * a + 128].reshape(2, 256, 128) for a in range(3)
+        ]
+
+    def back_pair(u, carry):
+        parts = three_taps(u, g_full, rows_back, 0, lambda b: 2 - b)
+        for a in range(3):
+            at = pl.ds(2 * u + a, 2)
+            sums[at] = sums[at] + parts[a]
+        return carry
+
     def back_frame(t, carry):
-        total = None
-        for a in range(3):
-            for b in range(3):
-                window = g_full[t + 2 - a, 2 - b : 10 - b].reshape(256, WIDE)
-                term = dot(window, rows_back[3 * a + b])
-                total = term if total is None else total + term
+        total = sums[t + 2]
         parts = total.reshape(8, 4, 8, 128)
         at = pl.ds(pl.multiple_of(64 * t, 64), 64)
         own = jnp.zeros((64, 128), F32)
@@ -567,9 +578,11 @@
         back_ref[at, :] = own
         return carry
 
-    lax.fori_loop(0, 5, back_frame, 0)
+    sums[...] = jnp.zeros((10, 256, 128), F32)
+    lax.fori_loop(0, 4, back_pair, 0)
+    lax.fori_loop(0, 4, back_frame, 0)
     relay(4, h_all, h_copies)
-    lax.fori_loop(5, 8, back_frame, 0)
+    lax.fori_loop(4, 8, back_frame, 0)
     p_copies = []
     for s in range(1, 4):
         to = (chip + s) % 4
@@ -597,18 +610,22 @@
     lax.fori_loop(0, 2, fill_hidden, 0)
     kept.append(keep(5, h_full, h_out))
 
+    def conv_pair(u, carry):
+        parts = three_taps(u, h_full, rows_fwd, 2, lambda b: b)
+        for a in range(3):
+            at = pl.ds(2 * u + 2 - a, 2)
+            sums[at] = sums[at] + parts[a]
+        return carry
+
     def conv_frame(t, carry):
-        total = None
-        for a in range(3):
-            for b in range(3):
-                window = h_full[t + a, b : b + 8].reshape(256, WIDE)
-                term = dot_nt(window, rows_fwd[3 * a + b])
-                total = term if total is None else total + term
+        total = sums[t]
         folded = fold_taps(total, 8, (-1, 0, 1))
         at = pl.ds(pl.multiple_of(64 * t, 64), 64)
         r_all[me, at, :] = (mask_ref[at, :] * (cells[at, :] + folded)).astype(BF16)
         return carry
 
+    sums[...] = jnp.zeros((10, 256, 128), F32)
+    lax.fori_loop(0, 4, conv_pair, 0)
     lax.fori_loop(0, 8, conv_frame, 0)
     r_copies = spread_out(6, r_all)
 
@@ -632,6 +649,44 @@
     x_all[me] = x_send[me]
     x_copies = send_all(8, lambda to: x_send.at[to], x_all.at[me])
 
+    relay(6, r_all, r_copies)
+
+    def turn_frame(t, carry):
+        stack_t[t] = g_full[t, 1:9].reshape(256, WIDE).T
+        return carry
+
+    lax.fori_loop(0, 8, turn_frame, 0)
+    kept.append(keep(6, stack_t, stack_out))
+
+    complete(r_copies)
+
+    def fill_residual(t, carry):
+        r_full[pl.ds(4 * t, 4), 0:4] = assemble(r_all, t).reshape(4, 4, 2, 32, WIDE)
+        return carry
+
+    lax.fori_loop(0, 2, fill_residual, 0)
+    kept.append(keep(7, r_full, r_out))
+
+    def down_frame(t, carry):
+        total = None
+        for b in range(3):
+            window = r_full[t, b // 2 : b // 2 + 4, b % 2].reshape(128, WIDE)
+            term = dot(window, rows_down[b])
+            total = term if total is None else total + term
+        folded = fold_taps(total, 4, (0, 1, 2)).astype(BF16)
+        to_row = lax.broadcasted_iota(jnp.int32, (16, 32), 0)
+        from_row = lax.broadcasted_iota(jnp.int32, (16, 32), 1)
+        even = (from_row == to_row * 2).astype(F32).astype(BF16)
+        d_send[t] = dot(even, folded).astype(BF16)
+        return carry
+
+    lax.fori_loop(0, 8, down_frame, 0)
+
+    def frames_of(to):
+        return pl.ds(4 * (to % 2), 4)
+
+    d_all[me] = d_send[frames_of(me)]
+    d_copies = send_all(7, lambda to: d_send.at[frames_of(to)], d_all.at[me])
     def og_frame(t, carry):
         from_row = lax.broadcasted_iota(jnp.int32, (WIDE, WIDE), 0)
         to_lane = lax.broadcasted_iota(jnp.int32, (WIDE, WIDE), 1)
@@ -646,44 +701,6 @@
     lax.fori_loop(0, 8, og_frame, 0)
 
     kept.append(keep(4, og_stack_t, og_stack_out))
-    relay(6, r_all, r_copies)
-    def turn_frame(t, carry):
-        rows = g_full[t, 1:9].reshape(256, WIDE).astype(F32)
-        stack_t[t] = rows.T.astype(BF16)
-        return carry
-
-    lax.fori_loop(0, 8, turn_frame, 0)
-    kept.append(keep(6, stack_t, stack_out))
-
-    complete(r_copies)
-
-    def fill_residual(t, carry):
-        r_full[pl.ds(4 * t, 4), 0:4] = assemble(r_all, t).reshape(4, 4, 2, 32, WIDE)
-        return carry
-
-    lax.fori_loop(0, 2, fill_residual, 0)
-    kept.append(keep(7, r_full, r_out))
-
-    def down_frame(t, carry):
-        total = None
-        for b in range(3):
-            window = r_full[t, b // 2 : b // 2 + 4, b % 2].reshape(128, WIDE)
-            term = dot_nt(window, rows_fwd[9 + b])
-            total = term if total is None else total + term
-        folded = fold_taps(total, 4, (0, 1, 2)).astype(BF16)
-        to_row = lax.broadcasted_iota(jnp.int32, (16, 32), 0)
-        from_row = lax.broadcasted_iota(jnp.int32, (16, 32), 1)
-        even = (from_row == to_row * 2).astype(F32).astype(BF16)
-        d_send[t] = dot(even, folded).astype(BF16)
-        return carry
-
-    lax.fori_loop(0, 8, down_frame, 0)
-
-    def frames_of(to):
-        return pl.ds(4 * (to % 2), 4)
-
-    d_all[me] = d_send[frames_of(me)]
-    d_copies = send_all(7, lambda to: d_send.at[frames_of(to)], d_all.at[me])
     arrived(x_copies)
     arrived(d_copies)
     for copy in kept:
@@ -797,9 +814,11 @@
             full,
             full,
             pltpu.VMEM((8, 5, 2, 32, WIDE), BF16),
-            pltpu.VMEM((9, 256, 128), BF16),
+            pltpu.VMEM((3, 256, 384), BF16),
+            pltpu.VMEM((3, 256, 128), BF16),
+            pltpu.VMEM((10, 256, 128), F32),
             pltpu.VMEM((8, 4, 32, WIDE), BF16),
-            pltpu.VMEM((12, 128, WIDE), BF16),
+            pltpu.VMEM((3, 256, 384), BF16),
             wide,
             wide,
             wide,

time: 55.6 us -> 54.8 us (0.986)
  Pallas kernels: 53.5 us -> 52.7 us
    pallas_call x1, Pallas kernels: 47.3 us -> 46.4 us  [fused(): pl.pallas_call(block_kernel, out_shape=(sent, sent_down, full_cells, even...]
where the time goes in v5:
time: 54.8 us; the launch traced here: 54.6 us
  Pallas kernels  52.7 us (96%)
  between operations  1.93 us (4%)
    pallas_call x1, Pallas kernels, fused(): pl.pallas_call(block_kernel, out_shape=(sent, sent_down, full_cells, even...  46.4 us
    pallas_call x1, Pallas kernels, fused(): pl.pallas_call(finish_kernel, out_shape=(jax.ShapeDtypeStruct(out_grad.sh...  6.27 us

profile of v5, /device:TPU:0, one launch (start us, length us, event | category | flops | bytes accessed | tf_op | source)
XLA Modules:
  0.0 54.6 jit_solution(16482981897818762476)
XLA Ops:
  1.9 46.4 %shard_map.120 = (bf16[8,64,128]{2,1,0:T(8,128)(2,1)}, bf16[8,4,16,128]{3,2,1,0:T(8,128)(2,1)}, bf16[10,10,32,256]{3,2,1,0:T(8,128)(2,1)}, bf16[8,5,2,32,256]{4,...) custom-call(s32[1]{0:T(128)S(6)} %copy.13.bucket_ref, s32[1]{0:T(128)S(6)} %copy.14.start_ref, ...), custom_call_target="tpu_custom_call" | custom-call | tf_op jit(solution)/shard_map/pallas_call | solution.py:790
  48.3 6.3 %shard_map.121 = (bf16[1,4,4,4,256]{4,3,2,1,0:T(4,128)(2,1)}, bf16[256,256]{1,0:T(8,128)(2,1)}, f32[64,6912]{1,0:T(8,128)}, f32[64,2304]{1,0:T(8,128)}) custom-call(bf16[8,64,128]{2,1,0:T(8,128)(2,1)} %get-tuple-element.14.x_hbm, bf16[8,4,16,128]{3,2,1,0:T(8,128)(2,1)} %get-tuple-element.15.d_hbm, bf16[10,10,32,256]{3,2,1,0:T(8,128)(2,1)} %get-tuple-element.16.h_hbm, ...), custom_call_target="tpu_custom_call" | custom-call | tf_op jit(solution)/shard_map/pallas_call | solution.py:848

commit v6 on v5

--- a/solution.py
+++ b/solution.py
@@ -257,14 +257,14 @@
     if distance == 0:
         return block
     rows = block.shape[0]
-    col = lax.broadcasted_iota(jnp.int32, block.shape, 0) % 8 + distance
+    col = (lax.broadcasted_iota(jnp.int32, block.shape, 0) & 7) + distance
     turned = pltpu.roll(block, (-distance) % rows, 0)
     return jnp.where((col >= 0) & (col < 8), turned, 0.0)
 
 
 def fold_taps(result, outer, distances):
     parts = result.reshape(outer, 4, 8, 128)
-    place = lax.broadcasted_iota(jnp.int32, (outer * 8, 128), 1) // OWN
+    place = lax.broadcasted_iota(jnp.int32, (outer * 8, 128), 1) >> 5
     total = None
     for tap in range(3):
         layer = jnp.zeros((outer * 8, 128), F32)
@@ -280,8 +280,8 @@
 
 
 def group_total(row):
-    first = lax.broadcasted_iota(jnp.int32, (128, 128), 0) // 8
-    second = lax.broadcasted_iota(jnp.int32, (128, 128), 1) // 8
+    first = lax.broadcasted_iota(jnp.int32, (128, 128), 0) >> 3
+    second = lax.broadcasted_iota(jnp.int32, (128, 128), 1) >> 3
     same = (first == second).astype(F32)
     wide = jnp.broadcast_to(row, (8, 128))
     return jnp.dot(wide, same, preferred_element_type=F32, precision=lax.Precision.HIGHEST)[0:1]
@@ -412,8 +412,44 @@
         to = (chip + s) % 4
         dw_copies.append(send(2, s, w_send.at[to], w_all.at[chip], to * 2 + core))
 
+    loads["cw"].wait()
+    from_row = lax.broadcasted_iota(jnp.int32, (WIDE, 128), 0)
+    to_lane = lax.broadcasted_iota(jnp.int32, (WIDE, 128), 1)
+    chosen = from_row == (to_lane >> 5) * 64 + OWN * core + (to_lane & 31)
+    chosen = chosen.astype(F32).astype(BF16)
+    for ab in range(9):
+        at = [(3 * ab + tap) * WIDE for tap in range(3)]
+        rows = jnp.concatenate([cw_ref[:, low : low + WIDE] for low in at], axis=0)
+        low = 128 * (ab // 3)
+        rows_back[ab % 3, 0:192, low : low + 128] = dot(rows, chosen).astype(BF16)
+        rows_back[ab % 3, 192:256, low : low + 128] = jnp.zeros((64, 128), BF16)
+
+    mine = pl.ds(pl.multiple_of(core * OWN, OWN), OWN)
+    blank = jnp.zeros((32, WIDE), BF16)
+
+    def turned(ref, block):
+        rows = [ref[mine, (3 * block + c) * WIDE : (3 * block + c + 1) * WIDE] for c in range(3)]
+        return jnp.concatenate(rows + [blank], axis=0).T
+
+    for ab in range(9):
+        low = 128 * (ab // 3)
+        rows_fwd[ab % 3, :, low : low + 128] = turned(cw_ref, ab)
+    for b in range(3):
+        rows_down[b] = turned(dw_ref, b)
+
+    sums[...] = jnp.zeros((10, 256, 128), F32)
+    edge = jnp.zeros((10, 32, WIDE), BF16)
+    for t in range(2):
+        h_full[t] = edge
+        g_full[8 + t] = edge
+    for t in range(8):
+        for full, off in ((h_full, 2), (g_full, 0)):
+            full[t + off, 0] = jnp.zeros((32, WIDE), BF16)
+            full[t + off, 9] = jnp.zeros((32, WIDE), BF16)
+        r_full[t, 4, 0] = jnp.zeros((32, WIDE), BF16)
+
     arrived(meta_copies)
-    place1 = lax.broadcasted_iota(jnp.int32, (1, 128), 1) // OWN
+    place1 = lax.broadcasted_iota(jnp.int32, (1, 128), 1) >> 5
     start = jnp.zeros((1, 128), F32)
     high = jnp.zeros((1, 128), F32)
     width = jnp.zeros((1, 128), F32)
@@ -423,12 +459,13 @@
         width = jnp.where(place1 == clip, meta_all[clip, 2:3, :], width)
     count = (8.0 - start) * high * width * 8.0
     row_id = lax.broadcasted_iota(jnp.int32, (512, 128), 0)
-    in_time = (row_id // 64).astype(F32) >= start
-    in_rows = (row_id // 8 % 8).astype(F32) < high
-    in_cols = (row_id % 8).astype(F32) < width
+    in_time = (row_id >> 6).astype(F32) >= start
+    in_rows = ((row_id >> 3) & 7).astype(F32) < high
+    in_cols = (row_id & 7).astype(F32) < width
     mask_ref[...] = jnp.where(in_time & in_rows & in_cols, 1.0, 0.0)
 
     arrived(v_copies)
+    relay(1, og_all, og_copies)
     stacked = jnp.concatenate(
         [
             jnp.concatenate([v_all[2 * other + c] for other in range(4)], axis=1)
@@ -450,11 +487,10 @@
     h_all[me] = (mask * (normed / (1.0 + jnp.exp(-normed)))).astype(BF16)
     h_copies = spread_out(4, h_all)
 
-    relay(1, og_all, og_copies)
     complete(og_copies)
     up_row = lax.broadcasted_iota(jnp.int32, (128, 64), 0)
     up_col = lax.broadcasted_iota(jnp.int32, (128, 64), 1)
-    lift = ((up_row // 8 == up_col // 4) & (up_row % 8 == 2 * (up_col % 4))).astype(F32).astype(BF16)
+    lift = ((up_row >> 3 == up_col >> 2) & ((up_row & 7) == 2 * (up_col & 3))).astype(F32).astype(BF16)
     for c in range(2):
         raised = [dot(lift, og_all[2 * clip + c]).reshape(16, 8, WIDE) for clip in range(4)]
         og_up[4 * c : 4 * c + 4] = (
@@ -480,43 +516,30 @@
     lax.fori_loop(0, 8, res_grad_frame, 0)
     g_copies = [send(5, 0, g_all.at[me], g_all.at[me], sibling)]
 
-    loads["cw"].wait()
-    from_row = lax.broadcasted_iota(jnp.int32, (WIDE, 128), 0)
-    to_lane = lax.broadcasted_iota(jnp.int32, (WIDE, 128), 1)
-    chosen = from_row == to_lane // OWN * 64 + OWN * core + to_lane % OWN
-    chosen = chosen.astype(F32).astype(BF16)
-    for ab in range(9):
-        at = [(3 * ab + tap) * WIDE for tap in range(3)]
-        rows = jnp.concatenate([cw_ref[:, low : low + WIDE] for low in at], axis=0)
-        low = 128 * (ab // 3)
-        rows_back[ab % 3, 0:192, low : low + 128] = dot(rows, chosen).astype(BF16)
-        rows_back[ab % 3, 192:256, low : low + 128] = jnp.zeros((64, 128), BF16)
-
-    mine = pl.ds(pl.multiple_of(core * OWN, OWN), OWN)
-    blank = jnp.zeros((32, WIDE), BF16)
-
-    def turned(ref, block):
-        rows = [ref[mine, (3 * block + c) * WIDE : (3 * block + c + 1) * WIDE] for c in range(3)]
-        return jnp.concatenate(rows + [blank], axis=0).T
-
-    for ab in range(9):
-        low = 128 * (ab // 3)
-        rows_fwd[ab % 3, :, low : low + 128] = turned(cw_ref, ab)
-    for b in range(3):
-        rows_down[b] = turned(dw_ref, b)
-
-    edge = jnp.zeros((10, 32, WIDE), BF16)
-    for t in range(2):
-        h_full[t] = edge
-        g_full[8 + t] = edge
-    for t in range(8):
-        for full, off in ((h_full, 2), (g_full, 0)):
-            full[t + off, 0] = jnp.zeros((32, WIDE), BF16)
-            full[t + off, 9] = jnp.zeros((32, WIDE), BF16)
-        r_full[t, 4, 0] = jnp.zeros((32, WIDE), BF16)
-
+    def keep(index, source, target):
+        copy = pltpu.make_async_copy(source, target, load_sems.at[index])
+        copy.start()
+        return copy
+
+    kept = []
+
+    from_row = lax.broadcasted_iota(jnp.int32, (WIDE, WIDE), 0)
+    to_lane = lax.broadcasted_iota(jnp.int32, (WIDE, WIDE), 1)
+    own_rows = (from_row == (to_lane & 63) + 64 * chip).astype(F32).astype(BF16)
+
+    def og_frame(t, carry):
+        rows = dot(og_up[t].reshape(128, WIDE), own_rows)
+        tap = lax.broadcasted_iota(jnp.int32, (128, WIDE), 1) >> 6
+        once, twice = move_cols(rows, -1), move_cols(rows, -2)
+        rows = jnp.where(tap == 0, rows, jnp.where(tap == 1, once, twice))
+        og_stack_t[t] = rows.T.astype(BF16)
+        return carry
+
+    lax.fori_loop(0, 8, og_frame, 0)
+
+    kept.append(keep(4, og_stack_t, og_stack_out))
     arrived(g_copies)
-    place = lax.broadcasted_iota(jnp.int32, (64, 128), 1) // OWN
+    place = lax.broadcasted_iota(jnp.int32, (64, 128), 1) >> 5
 
     def stack_frame(t, carry):
         at = pl.ds(pl.multiple_of(64 * t, 64), 64)
@@ -578,11 +601,9 @@
         back_ref[at, :] = own
         return carry
 
-    sums[...] = jnp.zeros((10, 256, 128), F32)
     lax.fori_loop(0, 4, back_pair, 0)
-    lax.fori_loop(0, 4, back_frame, 0)
     relay(4, h_all, h_copies)
-    lax.fori_loop(4, 8, back_frame, 0)
+    lax.fori_loop(0, 8, back_frame, 0)
     p_copies = []
     for s in range(1, 4):
         to = (chip + s) % 4
@@ -593,13 +614,6 @@
         clips = gathered_lanes([source[d, at, :] for d in range(8)], swap_ref[...])
         blocks = [clip.reshape(32, 8, WIDE) for clip in clips]
         return jnp.concatenate(blocks, axis=1).astype(BF16).reshape(4, 8, 32, WIDE)
-
-    def keep(index, source, target):
-        copy = pltpu.make_async_copy(source, target, load_sems.at[index])
-        copy.start()
-        return copy
-
-    kept = []
 
     complete(h_copies)
 
@@ -655,8 +669,7 @@
         stack_t[t] = g_full[t, 1:9].reshape(256, WIDE).T
         return carry
 
-    lax.fori_loop(0, 8, turn_frame, 0)
-    kept.append(keep(6, stack_t, stack_out))
+    lax.fori_loop(0, 4, turn_frame, 0)
 
     complete(r_copies)
 
@@ -687,20 +700,9 @@
 
     d_all[me] = d_send[frames_of(me)]
     d_copies = send_all(7, lambda to: d_send.at[frames_of(to)], d_all.at[me])
-    def og_frame(t, carry):
-        from_row = lax.broadcasted_iota(jnp.int32, (WIDE, WIDE), 0)
-        to_lane = lax.broadcasted_iota(jnp.int32, (WIDE, WIDE), 1)
-        chosen = (from_row == to_lane % 64 + 64 * chip).astype(F32).astype(BF16)
-        rows = dot(og_up[t].reshape(128, WIDE), chosen)
-        tap = lax.broadcasted_iota(jnp.int32, (128, WIDE), 1) // 64
-        once, twice = move_cols(rows, -1), move_cols(rows, -2)
-        rows = jnp.where(tap == 0, rows, jnp.where(tap == 1, once, twice))
-        og_stack_t[t] = rows.T.astype(BF16)
-        return carry
-
-    lax.fori_loop(0, 8, og_frame, 0)
-
-    kept.append(keep(4, og_stack_t, og_stack_out))
+    lax.fori_loop(4, 8, turn_frame, 0)
+    kept.append(keep(6, stack_t, stack_out))
+
     arrived(x_copies)
     arrived(d_copies)
     for copy in kept:

time: 54.8 us -> 55.6 us (1.015)
  Pallas kernels: 52.7 us -> 53.4 us
    pallas_call x1, Pallas kernels: 46.4 us -> 47.2 us  [fused(): pl.pallas_call(block_kernel, out_shape=(sent, sent_down, full_cells, even...]
where the time goes in v6:
time: 55.6 us; the launch traced here: 55.4 us
  Pallas kernels  53.4 us (96%)
  between operations  1.93 us (3%)
    pallas_call x1, Pallas kernels, fused(): pl.pallas_call(block_kernel, out_shape=(sent, sent_down, full_cells, even...  47.2 us
    pallas_call x1, Pallas kernels, fused(): pl.pallas_call(finish_kernel, out_shape=(jax.ShapeDtypeStruct(out_grad.sh...  6.27 us

profile of v6, /device:TPU:0, one launch (start us, length us, event | category | flops | bytes accessed | tf_op | source)
XLA Modules:
  0.0 55.4 jit_solution(849785038401453672)
XLA Ops:
  1.9 47.2 %shard_map.120 = (bf16[8,64,128]{2,1,0:T(8,128)(2,1)}, bf16[8,4,16,128]{3,2,1,0:T(8,128)(2,1)}, bf16[10,10,32,256]{3,2,1,0:T(8,128)(2,1)}, bf16[8,5,2,32,256]{4,...) custom-call(s32[1]{0:T(128)S(6)} %copy.13.bucket_ref, s32[1]{0:T(128)S(6)} %copy.14.start_ref, ...), custom_call_target="tpu_custom_call" | custom-call | tf_op jit(solution)/shard_map/pallas_call | solution.py:792
  49.1 6.3 %shard_map.121 = (bf16[1,4,4,4,256]{4,3,2,1,0:T(4,128)(2,1)}, bf16[256,256]{1,0:T(8,128)(2,1)}, f32[64,6912]{1,0:T(8,128)}, f32[64,2304]{1,0:T(8,128)}) custom-call(bf16[8,64,128]{2,1,0:T(8,128)(2,1)} %get-tuple-element.14.x_hbm, bf16[8,4,16,128]{3,2,1,0:T(8,128)(2,1)} %get-tuple-element.15.d_hbm, bf16[10,10,32,256]{3,2,1,0:T(8,128)(2,1)} %get-tuple-element.16.h_hbm, ...), custom_call_target="tpu_custom_call" | custom-call | tf_op jit(solution)/shard_map/pallas_call | solution.py:850

commit v7 on v6

--- a/solution.py
+++ b/solution.py
@@ -342,19 +342,22 @@
     def send_all(phase, source, target):
         return [send(phase, s, source((me + s) % 8), target, (me + s) % 8) for s in range(1, 8)]
 
-    def spread_out(phase, target):
-        copies = [send(phase, 4, target.at[me], target.at[me], sibling)]
+    def spread_out(phase, target, part):
+        block = target.at[me, part]
+        copies = [send(phase, 4, block, block, sibling)]
         for s in range(1, 4):
-            copies.append(send(phase, s, target.at[me], target.at[me], ((chip + s) % 4) * 2 + core))
+            copies.append(send(phase, s, block, block, ((chip + s) % 4) * 2 + core))
         return copies
 
-    def relay(phase, target, copies):
+    def relay(phase, target, part, copies):
         passed = []
         for s in range(1, 4):
             copies[s].wait_recv()
-            slot = ((chip + 4 - s) % 4) * 2 + core
-            passed.append(send(phase, 4 + s, target.at[slot], target.at[slot], sibling))
+            block = target.at[((chip + 4 - s) % 4) * 2 + core, part]
+            passed.append(send(phase, 4 + s, block, block, sibling))
         copies.extend(passed)
+
+    early, late = pl.ds(0, 256), pl.ds(256, 256)
 
     def complete(copies):
         copies[0].wait_recv()
@@ -393,7 +396,7 @@
     v_copies = send_all(0, lambda to: v_send.at[to], v_all.at[me])
     v_all[me] = v_send[me]
     og_all[me] = og_ref[0].astype(F32).reshape(64, WIDE).astype(BF16)
-    og_copies = spread_out(1, og_all)
+    og_copies = spread_out(1, og_all, pl.ds(0, 64))
 
     loads["dw"].wait()
     loads["pick"].wait()
@@ -465,7 +468,7 @@
     mask_ref[...] = jnp.where(in_time & in_rows & in_cols, 1.0, 0.0)
 
     arrived(v_copies)
-    relay(1, og_all, og_copies)
+    relay(1, og_all, pl.ds(0, 64), og_copies)
     stacked = jnp.concatenate(
         [
             jnp.concatenate([v_all[2 * other + c] for other in range(4)], axis=1)
@@ -485,7 +488,8 @@
     normed = offset * inverse
     normed_ref[...] = normed
     h_all[me] = (mask * (normed / (1.0 + jnp.exp(-normed)))).astype(BF16)
-    h_copies = spread_out(4, h_all)
+    h_copies = spread_out(4, h_all, early)
+    h_late = spread_out(11, h_all, late)
 
     complete(og_copies)
     up_row = lax.broadcasted_iota(jnp.int32, (128, 64), 0)
@@ -602,8 +606,9 @@
         return carry
 
     lax.fori_loop(0, 4, back_pair, 0)
-    relay(4, h_all, h_copies)
+    relay(4, h_all, early, h_copies)
     lax.fori_loop(0, 8, back_frame, 0)
+    relay(11, h_all, late, h_late)
     p_copies = []
     for s in range(1, 4):
         to = (chip + s) % 4
@@ -615,14 +620,11 @@
         blocks = [clip.reshape(32, 8, WIDE) for clip in clips]
         return jnp.concatenate(blocks, axis=1).astype(BF16).reshape(4, 8, 32, WIDE)
 
-    complete(h_copies)
 
     def fill_hidden(t, carry):
         h_full[pl.ds(4 * t + 2, 4), 1:9] = assemble(h_all, t)
         return carry
 
-    lax.fori_loop(0, 2, fill_hidden, 0)
-    kept.append(keep(5, h_full, h_out))
 
     def conv_pair(u, carry):
         parts = three_taps(u, h_full, rows_fwd, 2, lambda b: b)
@@ -639,11 +641,20 @@
         return carry
 
     sums[...] = jnp.zeros((10, 256, 128), F32)
-    lax.fori_loop(0, 4, conv_pair, 0)
-    lax.fori_loop(0, 8, conv_frame, 0)
-    r_copies = spread_out(6, r_all)
+    complete(h_copies)
+    fill_hidden(0, 0)
+    lax.fori_loop(0, 2, conv_pair, 0)
+    lax.fori_loop(0, 4, conv_frame, 0)
+    r_copies = spread_out(6, r_all, early)
+    complete(h_late)
+    fill_hidden(1, 0)
+    kept.append(keep(5, h_full, h_out))
+    lax.fori_loop(2, 4, conv_pair, 0)
+    lax.fori_loop(4, 8, conv_frame, 0)
+    r_late = spread_out(12, r_all, late)
 
     arrived(p_copies)
+    relay(6, r_all, early, r_copies)
     mask = mask_ref[...]
     normed = normed_ref[...]
     gate = 1.0 / (1.0 + jnp.exp(-normed))
@@ -663,7 +674,7 @@
     x_all[me] = x_send[me]
     x_copies = send_all(8, lambda to: x_send.at[to], x_all.at[me])
 
-    relay(6, r_all, r_copies)
+    relay(12, r_all, late, r_late)
 
     def turn_frame(t, carry):
         stack_t[t] = g_full[t, 1:9].reshape(256, WIDE).T
@@ -671,14 +682,9 @@
 
     lax.fori_loop(0, 4, turn_frame, 0)
 
-    complete(r_copies)
-
     def fill_residual(t, carry):
         r_full[pl.ds(4 * t, 4), 0:4] = assemble(r_all, t).reshape(4, 4, 2, 32, WIDE)
         return carry
-
-    lax.fori_loop(0, 2, fill_residual, 0)
-    kept.append(keep(7, r_full, r_out))
 
     def down_frame(t, carry):
         total = None
@@ -693,11 +699,17 @@
         d_send[t] = dot(even, folded).astype(BF16)
         return carry
 
-    lax.fori_loop(0, 8, down_frame, 0)
 
     def frames_of(to):
         return pl.ds(4 * (to % 2), 4)
 
+    complete(r_copies)
+    fill_residual(0, 0)
+    lax.fori_loop(0, 4, down_frame, 0)
+    complete(r_late)
+    fill_residual(1, 0)
+    kept.append(keep(7, r_full, r_out))
+    lax.fori_loop(4, 8, down_frame, 0)
     d_all[me] = d_send[frames_of(me)]
     d_copies = send_all(7, lambda to: d_send.at[frames_of(to)], d_all.at[me])
     lax.fori_loop(4, 8, turn_frame, 0)
@@ -708,7 +720,7 @@
     for copy in kept:
         copy.wait()
     for copies in (
-        meta_copies, v_copies, og_copies, dw_copies, p_copies, h_copies, g_copies, r_copies, x_copies,
+        meta_copies, v_copies, og_copies, dw_copies, p_copies, h_copies, h_late, g_copies, r_copies, r_late, x_copies,
         d_copies,
     ):
         for copy in copies:
@@ -829,8 +841,8 @@
             pltpu.VMEM((8, 256, 128), BF16),
             wide,
             pltpu.SemaphoreType.DMA((8,)),
-            pltpu.SemaphoreType.DMA((11, 8)),
-            pltpu.SemaphoreType.DMA((11, 8)),
+            pltpu.SemaphoreType.DMA((13, 8)),
+            pltpu.SemaphoreType.DMA((13, 8)),
         ],
         compiler_params=pltpu.CompilerParams(
             collective_id=0, has_side_effects=True, vmem_limit_bytes=60 * 2**20

time: 55.6 us -> 55.2 us (level)
  no operation moved by 1% of the time
where the time goes in v7:
time: 55.2 us; the launch traced here: 55 us
  Pallas kernels  53.1 us (96%)
  between operations  1.93 us (3%)
    pallas_call x1, Pallas kernels, fused(): pl.pallas_call(block_kernel, out_shape=(sent, sent_down, full_cells, even...  46.8 us
    pallas_call x1, Pallas kernels, fused(): pl.pallas_call(finish_kernel, out_shape=(jax.ShapeDtypeStruct(out_grad.sh...  6.27 us

profile of v7, /device:TPU:0, one launch (start us, length us, event | category | flops | bytes accessed | tf_op | source)
XLA Modules:
  0.0 55.0 jit_solution(17441568167585457551)
XLA Ops:
  1.9 46.8 %shard_map.120 = (bf16[8,64,128]{2,1,0:T(8,128)(2,1)}, bf16[8,4,16,128]{3,2,1,0:T(8,128)(2,1)}, bf16[10,10,32,256]{3,2,1,0:T(8,128)(2,1)}, bf16[8,5,2,32,256]{4,...) custom-call(s32[1]{0:T(128)S(6)} %copy.13.bucket_ref, s32[1]{0:T(128)S(6)} %copy.14.start_ref, ...), custom_call_target="tpu_custom_call" | custom-call | tf_op jit(solution)/shard_map/pallas_call | solution.py:804
  48.7 6.3 %shard_map.121 = (bf16[1,4,4,4,256]{4,3,2,1,0:T(4,128)(2,1)}, bf16[256,256]{1,0:T(8,128)(2,1)}, f32[64,6912]{1,0:T(8,128)}, f32[64,2304]{1,0:T(8,128)}) custom-call(bf16[8,64,128]{2,1,0:T(8,128)(2,1)} %get-tuple-element.14.x_hbm, bf16[8,4,16,128]{3,2,1,0:T(8,128)(2,1)} %get-tuple-element.15.d_hbm, bf16[10,10,32,256]{3,2,1,0:T(8,128)(2,1)} %get-tuple-element.16.h_hbm, ...), custom_call_target="tpu_custom_call" | custom-call | tf_op jit(solution)/shard_map/pallas_call | solution.py:862
